TPU v7x, 256 devices: a whole 4x4x8 slice. The times are simulated.
256 devices in a mesh: probe: 32 (over z, x_hi, core), depth: 8 (over y, x_lo).
Axes of the slice: x: 4 (x_hi: 2, x_lo: 2; x = x_hi * 2 + x_lo), y: 4, z: 8, core: 2. Of those that a mesh axis runs over, the one named last changes fastest.
Arguments:
- potential: float32 [16, 4096, 1024], P('depth', 'probe'), may hold values from -6 to 6
- probe: float32 [2, 256, 256], replicated, may hold values from -6 to 6
- positions: int32 [32, 2], P('probe'), may hold values from 0 to 4095, as said below
- intensity: float32 [32, 256, 256], P('probe'), may hold values from 0 to 4
Outputs:
- potential_grad: float32 [16, 4096, 1024], P('depth', 'probe')
Inputs may be any that keep to these rules, and one draw needn't show every extreme that they name: `positions`: entry 0 of probe p is the top row of its window and entry 1 its left column, 0 to 768. The window's centre row, (entry 128) mod 4096, lies in rows g * 128 to g * 128 + 127, where g = p // 1 is the probe's group.
All inputs are finite; a program needn't handle non-finite values.
Results may differ from a plain program's by a relative error of at most 0.0003.
Values sent between devices are 32-bit elements; how exact they have to be, the bound alone decides.
A program may use at most 64 MiB of HBM per device.

v0:
```python
import jax
import jax.numpy as jnp
from jax import lax
from jax.sharding import PartitionSpec as P

interaction = 0.5
fresnel_phase = 60.0
highest = lax.Precision.HIGHEST


def extended_2(block, sides, width):
    for axis, dim in sides:
        count = lax.axis_size(axis)
        forward = [(i, i + 1) for i in range(count - 1)]
        forward.append((count - 1, 0))
        backward = [(target, source) for source, target in forward]
        low = lax.ppermute(
            lax.slice_in_dim(block, block.shape[dim] - width, None, axis=dim), axis, forward
        )
        high = lax.ppermute(lax.slice_in_dim(block, 0, width, axis=dim), axis, backward)
        block = jnp.concatenate([low, block, high], axis=dim)
    return block


def shifted(shard, axis, by):
    peers = lax.axis_size(axis)
    pairs = [(i, i + by) for i in range(peers) if 0 <= i + by < peers]
    return lax.ppermute(shard, axis, pairs)


def passed_along(value, axis, steps):
    count = lax.axis_size(axis)
    pairs = [(source, (source + steps) % count) for source in range(count)]
    return lax.ppermute(value, axis, pairs)


def dft_tables(extent):
    counter = jnp.arange(extent, dtype=jnp.int32)
    product = counter[:, None] * counter[None, :] % extent
    angles = 2.0 * jnp.pi / extent * product.astype(jnp.float32)
    norm_scale = 1.0 / jnp.sqrt(jnp.float32(extent))
    return (jnp.cos(angles) * norm_scale, -jnp.sin(angles) * norm_scale)


def kernel_table(extent):
    counter = jnp.arange(extent, dtype=jnp.int32)
    frequency = ((counter + extent // 2) % extent - extent // 2).astype(jnp.float32) / extent
    phases = -fresnel_phase * (frequency[:, None] ** 2 + frequency[None, :] ** 2)
    return (jnp.cos(phases), jnp.sin(phases))


def left_product(matrix, field):
    return jnp.einsum("jk,...kl->...jl", matrix, field, precision=highest)


def right_product(field, matrix):
    return jnp.einsum("...jk,kl->...jl", field, matrix, precision=highest)


def complex_left(matrices, fields):
    return (
        left_product(matrices[0], fields[0]) - left_product(matrices[1], fields[1]),
        left_product(matrices[0], fields[1]) + left_product(matrices[1], fields[0]),
    )


def complex_right(fields, matrices):
    return (
        right_product(fields[0], matrices[0]) - right_product(fields[1], matrices[1]),
        right_product(fields[0], matrices[1]) + right_product(fields[1], matrices[0]),
    )


def forward_dft(fields, tables):
    return complex_right(complex_left(tables, fields), tables)


def inverse_dft(fields, tables):
    conjugate = (tables[0], -tables[1])
    return complex_right(complex_left(conjugate, fields), conjugate)


def propagate(fields, tables, kernel):
    spectrum = forward_dft(fields, tables)
    moved = (
        kernel[0] * spectrum[0] - kernel[1] * spectrum[1],
        kernel[0] * spectrum[1] + kernel[1] * spectrum[0],
    )
    return inverse_dft(moved, tables)


def transmit(fields, window):
    cosine = jnp.cos(interaction * window)
    sine_part = jnp.sin(interaction * window)
    return (cosine * fields[0] - sine_part * fields[1], cosine * fields[1] + sine_part * fields[0])


def local(potential, probe, positions, intensity):
    layers, strip, columns = potential.shape
    extent = probe.shape[1]
    probes_here = positions.shape[0]
    group_id = lax.axis_index("probe")
    group_count = lax.axis_size("probe")
    depth_id = lax.axis_index("depth")
    depth_count = lax.axis_size("depth")
    total_rows = strip * group_count
    is_first = depth_id == 0
    is_last = depth_id == depth_count - 1
    tables = dft_tables(extent)
    kernel = kernel_table(extent)
    back_kernel = (kernel[0], -kernel[1])
    extended = extended_2(potential, (("probe", 1),), strip)
    local_rows = (positions[:, 0] - (group_id - 1) * strip) % total_rows
    local_columns = positions[:, 1]

    def cut_window(row_start, column_start):
        return lax.dynamic_slice(extended, (0, row_start, column_start), (layers, extent, extent))

    windows = jax.vmap(cut_window)(local_rows, local_columns)
    blocks = probes_here // probes_here

    def slab_forward(fields, block_windows):
        current = (fields[:, 0], fields[:, 1])
        saved_list = []
        for layer_id in range(layers):
            current = transmit(current, block_windows[:, layer_id])
            saved_list.append(jnp.stack(current, axis=1))
            current = propagate(current, tables, kernel)
        return (jnp.stack(current, axis=1), jnp.stack(saved_list, axis=1))

    def slab_backward(fields, block_saved, block_windows):
        current = (fields[:, 0], fields[:, 1])
        grad_list = []
        for layer_id in reversed(range(layers)):
            current = propagate(current, tables, back_kernel)
            saved_real = block_saved[:, layer_id, 0]
            saved_imag = block_saved[:, layer_id, 1]
            grad_list.append(interaction * (current[1] * saved_real - current[0] * saved_imag))
            cosine = jnp.cos(interaction * block_windows[:, layer_id])
            sine_part = jnp.sin(interaction * block_windows[:, layer_id])
            current = (
                cosine * current[0] + sine_part * current[1],
                cosine * current[1] - sine_part * current[0],
            )
        return (jnp.stack(current, axis=1), jnp.stack(grad_list[::-1], axis=1))

    start_field = probe[None]
    empty_wave = jnp.zeros((probes_here, 2, extent, extent), jnp.float32)
    stored = jnp.zeros((probes_here, layers, 2, extent, extent), jnp.float32)
    exits = jnp.zeros((probes_here, 2, extent, extent), jnp.float32)

    def forward_step(counter, state_carry):
        wave_in, stored, exits = state_carry
        block_id = counter - depth_id
        active = (block_id >= 0) & (block_id < blocks)
        first_row = jnp.clip(block_id, 0, blocks - 1) * probes_here
        incoming = jnp.where(is_first, start_field, wave_in)

        def forward_process(operands):
            fields, stored_in, exits_in = operands
            outgoing, saved = slab_forward(fields, windows)
            stored_out = lax.dynamic_update_slice_in_dim(stored_in, saved, first_row, 0)
            return (outgoing, stored_out, outgoing)

        def forward_passing(operands):
            return operands

        outgoing, stored, exits = lax.cond(
            active, forward_process, forward_passing, (incoming, stored, exits)
        )
        wave_next = shifted(outgoing, "depth", 1)
        return (wave_next, stored, exits)

    unused_wave, stored, exits = lax.fori_loop(
        0, blocks + depth_count - 1, forward_step, (empty_wave, stored, exits)
    )

    def detector(exit_fields):
        far_field = forward_dft((exit_fields[:, 0], exit_fields[:, 1]), tables)
        misfit = far_field[0] * far_field[0] + far_field[1] * far_field[1] - intensity
        weighted = (misfit * far_field[0], misfit * far_field[1])
        return jnp.stack(inverse_dft(weighted, tables), axis=1)

    seed_grads = lax.cond(is_last, detector, jnp.zeros_like, exits)
    grads_all = jnp.zeros((probes_here, layers, extent, extent), jnp.float32)

    def backward_step(counter, state_carry):
        wave_in, grads_in = state_carry
        block_id = counter - (depth_count - 1 - depth_id)
        active = (block_id >= 0) & (block_id < blocks)
        first_row = jnp.clip(block_id, 0, blocks - 1) * probes_here
        incoming = jnp.where(is_last, seed_grads, wave_in)

        def backward_process(operands):
            fields, grads_acc = operands
            outgoing, block_grads = slab_backward(fields, stored, windows)
            return (outgoing, lax.dynamic_update_slice_in_dim(grads_acc, block_grads, first_row, 0))

        def backward_passing(operands):
            return operands

        outgoing, grads_out = lax.cond(
            active, backward_process, backward_passing, (incoming, grads_in)
        )
        wave_next = shifted(outgoing, "depth", -1)
        return (wave_next, grads_out)

    unused_back, grads_all = lax.fori_loop(
        0, blocks + depth_count - 1, backward_step, (empty_wave, grads_all)
    )

    def deposit(probe_id, running):
        row_start = local_rows[probe_id]
        column_start = local_columns[probe_id]
        present = lax.dynamic_slice(running, (0, row_start, column_start), (layers, extent, extent))
        return lax.dynamic_update_slice(
            running, present + grads_all[probe_id], (0, row_start, column_start)
        )

    gathered = lax.fori_loop(0, probes_here, deposit, jnp.zeros_like(extended))
    from_above = passed_along(gathered[:, :strip], "probe", -1)
    from_below = passed_along(gathered[:, 2 * strip :], "probe", 1)
    return gathered[:, strip : 2 * strip] + from_above + from_below


def solution(mesh):
    in_specs = (P("depth", "probe", None), P(), P("probe", None), P("probe", None, None))
    out_specs = P("depth", "probe", None)
    return jax.shard_map(local, mesh=mesh, in_specs=in_specs, out_specs=out_specs, check_vma=False)
```

profile of v0, /device:TPU:1, one launch (start us, length us, event | category | flops | bytes accessed | tf_op | source)
XLA Modules:
  0.0 780.0 jit_solution(9588546517657534559)
XLA Ops:
  0.0 4.1 collective-permute-start.2
  10.9 16.5 %collective-permute-done.2 = f32[2,128,1024]{2,1,0:T(8,128)S(1)} collective-permute-done((f32[2,128,1024]{2,1,0:T(8,128)}, f32[2,128,1024]{2,1,0:T(8,128)S(1)}, u32[]{:S(2)}, u32[]{:S(2)}) %collective-permute-start.2) | collective-permute-done | bytes 1048608 | tf_op jit(solution)/shard_map/ppermute | solution.py:17
  27.4 3.9 collective-permute-done.3
  33.9 241.5 %while.46 = (s32[]{:T(128)}, f32[1,2,256,256]{3,2,1,0:T(8,128)S(1)}, f32[1,2,2,256,256]{4,3,2,1,0:T(8,128)}, f32[1,2,256,256]{3,2,1,0:T(8,128)S(1)}, s32[]{:T(12...) while((s32[]{:T(128)}, ...), condition=%wide.region_3.4_spmd.clone.clone.clone, body=%wide.region_0.3_spmd.clone.clone.clone.sunk | while | flops 6447759360 | bytes 46925120 | solution.py:174
  35.4 28.8 %conditional.12 = ((f32[1,2,256,256]{3,2,1,0:T(8,128)}, f32[1,2,2,256,256]{4,3,2,1,0:T(8,128)}, f32[1,2,256,256]{3,2,1,0:T(8,128)S(1)})) conditional(s32[]{:T(128)} %convert_element_type.269, (f32[1,2,256,256]{3,2,1,0:T(8,128)}, f32[1,2,2,256,256]{4,3,2,1,0:T(8,128)}, f32[1,2,256,256]{3,2,1,0:T(8,128)S(1)}) %tuple.230, ...), branch_computations={%region_1.1_spmd, %region_2.2_spmd.clone} | conditional | flops 6446579712 | bytes 42467360 | solution.py:168
  65.4 6.4 collective-permute-done
  72.9 32.5 %collective-permute-start = (f32[1,2,256,256]{3,2,1,0:T(8,128)}, f32[1,2,256,256]{3,2,1,0:T(8,128)S(1)}, u32[]{:S(2)}, u32[]{:S(2)}) collective-permute-start(f32[1,2,256,256]{3,2,1,0:T(8,128)} %get-tuple-element.1518), channel_id=1, source_target_pairs={{0,1},{1,2},{2,3},{3,4},{4,5},{5,6},{6,7},{8,9},{9,10},{10,11},{11... | collective-permute-start | bytes 1572872 | tf_op jit(solution)/shard_map/while/body/eval_jaxpr/ppermute | solution.py:28
  105.4 7.5 collective-permute-done
  114.0 4.0 collective-permute-start
  118.0 6.4 collective-permute-done
  125.5 30.2 %collective-permute-start = (f32[1,2,256,256]{3,2,1,0:T(8,128)}, f32[1,2,256,256]{3,2,1,0:T(8,128)S(1)}, u32[]{:S(2)}, u32[]{:S(2)}) collective-permute-start(f32[1,2,256,256]{3,2,1,0:T(8,128)} %get-tuple-element.1518), channel_id=1, source_target_pairs={{0,1},{1,2},{2,3},{3,4},{4,5},{5,6},{6,7},{8,9},{9,10},{10,11},{11... | collective-permute-start | bytes 1572872 | tf_op jit(solution)/shard_map/while/body/eval_jaxpr/ppermute | solution.py:28
  155.7 6.4 collective-permute-done
  163.2 4.6 collective-permute-start
  167.9 7.0 collective-permute-done
  175.9 29.5 %collective-permute-start = (f32[1,2,256,256]{3,2,1,0:T(8,128)}, f32[1,2,256,256]{3,2,1,0:T(8,128)S(1)}, u32[]{:S(2)}, u32[]{:S(2)}) collective-permute-start(f32[1,2,256,256]{3,2,1,0:T(8,128)} %get-tuple-element.1518), channel_id=1, source_target_pairs={{0,1},{1,2},{2,3},{3,4},{4,5},{5,6},{6,7},{8,9},{9,10},{10,11},{11... | collective-permute-start | bytes 1572872 | tf_op jit(solution)/shard_map/while/body/eval_jaxpr/ppermute | solution.py:28
  205.4 7.5 collective-permute-done
  214.0 4.9 collective-permute-start
  218.9 8.5 %collective-permute-done = f32[1,2,256,256]{3,2,1,0:T(8,128)S(1)} collective-permute-done((f32[1,2,256,256]{3,2,1,0:T(8,128)}, f32[1,2,256,256]{3,2,1,0:T(8,128)S(1)}, u32[]{:S(2)}, u32[]{:S(2)}) %collective-permute-start) | collective-permute-done | bytes 524320 | tf_op jit(solution)/shard_map/while/body/eval_jaxpr/ppermute | solution.py:28
  228.6 30.1 %collective-permute-start = (f32[1,2,256,256]{3,2,1,0:T(8,128)}, f32[1,2,256,256]{3,2,1,0:T(8,128)S(1)}, u32[]{:S(2)}, u32[]{:S(2)}) collective-permute-start(f32[1,2,256,256]{3,2,1,0:T(8,128)} %get-tuple-element.1518), channel_id=1, source_target_pairs={{0,1},{1,2},{2,3},{3,4},{4,5},{5,6},{6,7},{8,9},{9,10},{10,11},{11... | collective-permute-start | bytes 1572872 | tf_op jit(solution)/shard_map/while/body/eval_jaxpr/ppermute | solution.py:28
  258.7 9.0 %collective-permute-done = f32[1,2,256,256]{3,2,1,0:T(8,128)S(1)} collective-permute-done((f32[1,2,256,256]{3,2,1,0:T(8,128)}, f32[1,2,256,256]{3,2,1,0:T(8,128)S(1)}, u32[]{:S(2)}, u32[]{:S(2)}) %collective-permute-start) | collective-permute-done | bytes 524320 | tf_op jit(solution)/shard_map/while/body/eval_jaxpr/ppermute | solution.py:28
  276.4 467.1 %while.47 = (s32[]{:T(128)}, f32[1,2,256,256]{3,2,1,0:T(8,128)S(1)}, f32[1,2,256,256]{3,2,1,0:T(8,128)}, s32[]{:T(128)}, pred[]{:T(512)}, /*index=5*/f32[1,2,256...) while((s32[]{:T(128)}, ...), condition=%wide.region_9.10_spmd.clone.clone.clone, body=%wide.region_6.9_spmd.clone.clone.clone.sunk | while | flops 6448611328 | bytes 45090104 | solution.py:208
  292.9 14.2 %collective-permute-done.1 = f32[1,2,256,256]{3,2,1,0:T(8,128)S(1)} collective-permute-done((f32[1,2,256,256]{3,2,1,0:T(8,128)S(1)}, f32[1,2,256,256]{3,2,1,0:T(8,128)S(1)}, u32[]{:S(2)}, u32[]{:S(2)}) %collective-permute-start.1) | collective-permute-done | bytes 524320 | tf_op jit(solution)/shard_map/while/body/eval_jaxpr/ppermute | solution.py:28
  308.7 37.8 %collective-permute-done.1 = f32[1,2,256,256]{3,2,1,0:T(8,128)S(1)} collective-permute-done((f32[1,2,256,256]{3,2,1,0:T(8,128)S(1)}, f32[1,2,256,256]{3,2,1,0:T(8,128)S(1)}, u32[]{:S(2)}, u32[]{:S(2)}) %collective-permute-start.1) | collective-permute-done | bytes 524320 | tf_op jit(solution)/shard_map/while/body/eval_jaxpr/ppermute | solution.py:28
  348.1 15.9 %collective-permute-done.1 = f32[1,2,256,256]{3,2,1,0:T(8,128)S(1)} collective-permute-done((f32[1,2,256,256]{3,2,1,0:T(8,128)S(1)}, f32[1,2,256,256]{3,2,1,0:T(8,128)S(1)}, u32[]{:S(2)}, u32[]{:S(2)}) %collective-permute-start.1) | collective-permute-done | bytes 524320 | tf_op jit(solution)/shard_map/while/body/eval_jaxpr/ppermute | solution.py:28
  365.6 40.3 %collective-permute-done.1 = f32[1,2,256,256]{3,2,1,0:T(8,128)S(1)} collective-permute-done((f32[1,2,256,256]{3,2,1,0:T(8,128)S(1)}, f32[1,2,256,256]{3,2,1,0:T(8,128)S(1)}, u32[]{:S(2)}, u32[]{:S(2)}) %collective-permute-start.1) | collective-permute-done | bytes 524320 | tf_op jit(solution)/shard_map/while/body/eval_jaxpr/ppermute | solution.py:28
  407.6 15.7 %collective-permute-done.1 = f32[1,2,256,256]{3,2,1,0:T(8,128)S(1)} collective-permute-done((f32[1,2,256,256]{3,2,1,0:T(8,128)S(1)}, f32[1,2,256,256]{3,2,1,0:T(8,128)S(1)}, u32[]{:S(2)}, u32[]{:S(2)}) %collective-permute-start.1) | collective-permute-done | bytes 524320 | tf_op jit(solution)/shard_map/while/body/eval_jaxpr/ppermute | solution.py:28
  424.9 38.8 %collective-permute-done.1 = f32[1,2,256,256]{3,2,1,0:T(8,128)S(1)} collective-permute-done((f32[1,2,256,256]{3,2,1,0:T(8,128)S(1)}, f32[1,2,256,256]{3,2,1,0:T(8,128)S(1)}, u32[]{:S(2)}, u32[]{:S(2)}) %collective-permute-start.1) | collective-permute-done | bytes 524320 | tf_op jit(solution)/shard_map/while/body/eval_jaxpr/ppermute | solution.py:28
  465.3 233.6 %collective-permute-done.1 = f32[1,2,256,256]{3,2,1,0:T(8,128)S(1)} collective-permute-done((f32[1,2,256,256]{3,2,1,0:T(8,128)S(1)}, f32[1,2,256,256]{3,2,1,0:T(8,128)S(1)}, u32[]{:S(2)}, u32[]{:S(2)}) %collective-permute-start.1) | collective-permute-done | bytes 524320 | tf_op jit(solution)/shard_map/while/body/eval_jaxpr/ppermute | solution.py:28
  699.1 31.7 %conditional.13 = ((f32[1,2,256,256]{3,2,1,0:T(8,128)S(1)}, f32[1,2,256,256]{3,2,1,0:T(8,128)})) conditional(s32[]{:T(128)} %convert_element_type.271, (f32[1,2,256,256]{3,2,1,0:T(8,128)S(1)}, f32[1,2,256,256]{3,2,1,0:T(8,128)}) %tuple.234, (f32[1,2,256,256]{3,2,1,0:T(8,128)S(1)}, f32[1,2,256,256]{3,2,1,0:T(8,128)S(1)}, ...), branch_computations={%region_7.7_spmd, %region_8.8_spmd.clone} | conditional | flops 6447431680 | bytes 40632344 | solution.py:202
  732.1 11.3 %collective-permute-done.1 = f32[1,2,256,256]{3,2,1,0:T(8,128)S(1)} collective-permute-done((f32[1,2,256,256]{3,2,1,0:T(8,128)S(1)}, f32[1,2,256,256]{3,2,1,0:T(8,128)S(1)}, u32[]{:S(2)}, u32[]{:S(2)}) %collective-permute-start.1) | collective-permute-done | bytes 524320 | tf_op jit(solution)/shard_map/while/body/eval_jaxpr/ppermute | solution.py:28
  744.0 7.3 dynamic_update_slice.6
  754.9 23.7 %collective-permute-done.4 = f32[2,128,1024]{2,1,0:T(8,128)S(1)} collective-permute-done((f32[2,128,1024]{2,1,0:T(8,128)S(1)}, f32[2,128,1024]{2,1,0:T(8,128)S(1)}, u32[]{:S(2)}, u32[]{:S(2)}) %collective-permute-start.4) | collective-permute-done | bytes 1048608 | tf_op jit(solution)/shard_map/ppermute | solution.py:34
  (169 shorter events, 93.2 us)
Async XLA Ops:
  0.0 33.9 %copy-start = (f32[2,256,256]{2,1,0:T(8,128)S(1)}, f32[2,256,256]{2,1,0:T(8,128)}, u32[]{:S(2)}) copy-start(f32[2,256,256]{2,1,0:T(8,128)} %param.15) | copy-start | bytes 1572868
  0.0 27.4 %collective-permute-start.2 = (f32[2,128,1024]{2,1,0:T(8,128)}, f32[2,128,1024]{2,1,0:T(8,128)S(1)}, u32[]{:S(2)}, u32[]{:S(2)}) collective-permute-start(f32[2,128,1024]{2,1,0:T(8,128)} %param.14), channel_id=1, source_target_pairs={{0,8},{8,16},{16,24},{24,32},{32,40},{40,48},{48,56},{56,64},{64,7... | collective-permute-start | bytes 3145736 | tf_op jit(solution)/shard_map/ppermute | solution.py:17
  4.1 27.2 %collective-permute-start.3 = (f32[2,128,1024]{2,1,0:T(8,128)}, f32[2,128,1024]{2,1,0:T(8,128)S(1)}, u32[]{:S(2)}, u32[]{:S(2)}) collective-permute-start(f32[2,128,1024]{2,1,0:T(8,128)} %param.14), channel_id=1, source_target_pairs={{8,0},{16,8},{24,16},{32,24},{40,32},{48,40},{56,48},{64,56},{72,6... | collective-permute-start | bytes 3145736 | tf_op jit(solution)/shard_map/ppermute | solution.py:20
  64.1 7.7 collective-permute-start
  72.9 39.9 %collective-permute-start = (f32[1,2,256,256]{3,2,1,0:T(8,128)}, f32[1,2,256,256]{3,2,1,0:T(8,128)S(1)}, u32[]{:S(2)}, u32[]{:S(2)}) collective-permute-start(f32[1,2,256,256]{3,2,1,0:T(8,128)} %get-tuple-element.1518), channel_id=1, source_target_pairs={{0,1},{1,2},{2,3},{3,4},{4,5},{5,6},{6,7},{8,9},{9,10},{10,11},{11... | collective-permute-start | bytes 1572872 | tf_op jit(solution)/shard_map/while/body/eval_jaxpr/ppermute | solution.py:28
  114.0 10.4 %collective-permute-start = (f32[1,2,256,256]{3,2,1,0:T(8,128)}, f32[1,2,256,256]{3,2,1,0:T(8,128)S(1)}, u32[]{:S(2)}, u32[]{:S(2)}) collective-permute-start(f32[1,2,256,256]{3,2,1,0:T(8,128)} %get-tuple-element.1518), channel_id=1, source_target_pairs={{0,1},{1,2},{2,3},{3,4},{4,5},{5,6},{6,7},{8,9},{9,10},{10,11},{11... | collective-permute-start | bytes 1572872 | tf_op jit(solution)/shard_map/while/body/eval_jaxpr/ppermute | solution.py:28
  125.5 36.6 %collective-permute-start = (f32[1,2,256,256]{3,2,1,0:T(8,128)}, f32[1,2,256,256]{3,2,1,0:T(8,128)S(1)}, u32[]{:S(2)}, u32[]{:S(2)}) collective-permute-start(f32[1,2,256,256]{3,2,1,0:T(8,128)} %get-tuple-element.1518), channel_id=1, source_target_pairs={{0,1},{1,2},{2,3},{3,4},{4,5},{5,6},{6,7},{8,9},{9,10},{10,11},{11... | collective-permute-start | bytes 1572872 | tf_op jit(solution)/shard_map/while/body/eval_jaxpr/ppermute | solution.py:28
  163.2 11.6 %collective-permute-start = (f32[1,2,256,256]{3,2,1,0:T(8,128)}, f32[1,2,256,256]{3,2,1,0:T(8,128)S(1)}, u32[]{:S(2)}, u32[]{:S(2)}) collective-permute-start(f32[1,2,256,256]{3,2,1,0:T(8,128)} %get-tuple-element.1518), channel_id=1, source_target_pairs={{0,1},{1,2},{2,3},{3,4},{4,5},{5,6},{6,7},{8,9},{9,10},{10,11},{11... | collective-permute-start | bytes 1572872 | tf_op jit(solution)/shard_map/while/body/eval_jaxpr/ppermute | solution.py:28
  175.9 37.0 %collective-permute-start = (f32[1,2,256,256]{3,2,1,0:T(8,128)}, f32[1,2,256,256]{3,2,1,0:T(8,128)S(1)}, u32[]{:S(2)}, u32[]{:S(2)}) collective-permute-start(f32[1,2,256,256]{3,2,1,0:T(8,128)} %get-tuple-element.1518), channel_id=1, source_target_pairs={{0,1},{1,2},{2,3},{3,4},{4,5},{5,6},{6,7},{8,9},{9,10},{10,11},{11... | collective-permute-start | bytes 1572872 | tf_op jit(solution)/shard_map/while/body/eval_jaxpr/ppermute | solution.py:28
  214.0 13.5 %collective-permute-start = (f32[1,2,256,256]{3,2,1,0:T(8,128)}, f32[1,2,256,256]{3,2,1,0:T(8,128)S(1)}, u32[]{:S(2)}, u32[]{:S(2)}) collective-permute-start(f32[1,2,256,256]{3,2,1,0:T(8,128)} %get-tuple-element.1518), channel_id=1, source_target_pairs={{0,1},{1,2},{2,3},{3,4},{4,5},{5,6},{6,7},{8,9},{9,10},{10,11},{11... | collective-permute-start | bytes 1572872 | tf_op jit(solution)/shard_map/while/body/eval_jaxpr/ppermute | solution.py:28
  228.6 39.2 %collective-permute-start = (f32[1,2,256,256]{3,2,1,0:T(8,128)}, f32[1,2,256,256]{3,2,1,0:T(8,128)S(1)}, u32[]{:S(2)}, u32[]{:S(2)}) collective-permute-start(f32[1,2,256,256]{3,2,1,0:T(8,128)} %get-tuple-element.1518), channel_id=1, source_target_pairs={{0,1},{1,2},{2,3},{3,4},{4,5},{5,6},{6,7},{8,9},{9,10},{10,11},{11... | collective-permute-start | bytes 1572872 | tf_op jit(solution)/shard_map/while/body/eval_jaxpr/ppermute | solution.py:28
  291.6 15.5 %collective-permute-start.1 = (f32[1,2,256,256]{3,2,1,0:T(8,128)S(1)}, f32[1,2,256,256]{3,2,1,0:T(8,128)S(1)}, u32[]{:S(2)}, u32[]{:S(2)}) collective-permute-start(f32[1,2,256,256]{3,2,1,0:T(8,128)S(1)} %get-tuple-element.1532), channel_id=1, source_target_pairs={{1,0},{2,1},{3,2},{4,3},{5,4},{6,5},{7,6},{9,8},{10,9},{11,10},{12... | collective-permute-start | bytes 1572872 | tf_op jit(solution)/shard_map/while/body/eval_jaxpr/ppermute | solution.py:28
  307.4 39.1 %collective-permute-start.1 = (f32[1,2,256,256]{3,2,1,0:T(8,128)S(1)}, f32[1,2,256,256]{3,2,1,0:T(8,128)S(1)}, u32[]{:S(2)}, u32[]{:S(2)}) collective-permute-start(f32[1,2,256,256]{3,2,1,0:T(8,128)S(1)} %get-tuple-element.1532), channel_id=1, source_target_pairs={{1,0},{2,1},{3,2},{4,3},{5,4},{6,5},{7,6},{9,8},{10,9},{11,10},{12... | collective-permute-start | bytes 1572872 | tf_op jit(solution)/shard_map/while/body/eval_jaxpr/ppermute | solution.py:28
  346.8 17.2 %collective-permute-start.1 = (f32[1,2,256,256]{3,2,1,0:T(8,128)S(1)}, f32[1,2,256,256]{3,2,1,0:T(8,128)S(1)}, u32[]{:S(2)}, u32[]{:S(2)}) collective-permute-start(f32[1,2,256,256]{3,2,1,0:T(8,128)S(1)} %get-tuple-element.1532), channel_id=1, source_target_pairs={{1,0},{2,1},{3,2},{4,3},{5,4},{6,5},{7,6},{9,8},{10,9},{11,10},{12... | collective-permute-start | bytes 1572872 | tf_op jit(solution)/shard_map/while/body/eval_jaxpr/ppermute | solution.py:28
  364.3 41.6 %collective-permute-start.1 = (f32[1,2,256,256]{3,2,1,0:T(8,128)S(1)}, f32[1,2,256,256]{3,2,1,0:T(8,128)S(1)}, u32[]{:S(2)}, u32[]{:S(2)}) collective-permute-start(f32[1,2,256,256]{3,2,1,0:T(8,128)S(1)} %get-tuple-element.1532), channel_id=1, source_target_pairs={{1,0},{2,1},{3,2},{4,3},{5,4},{6,5},{7,6},{9,8},{10,9},{11,10},{12... | collective-permute-start | bytes 1572872 | tf_op jit(solution)/shard_map/while/body/eval_jaxpr/ppermute | solution.py:28
  406.3 17.0 %collective-permute-start.1 = (f32[1,2,256,256]{3,2,1,0:T(8,128)S(1)}, f32[1,2,256,256]{3,2,1,0:T(8,128)S(1)}, u32[]{:S(2)}, u32[]{:S(2)}) collective-permute-start(f32[1,2,256,256]{3,2,1,0:T(8,128)S(1)} %get-tuple-element.1532), channel_id=1, source_target_pairs={{1,0},{2,1},{3,2},{4,3},{5,4},{6,5},{7,6},{9,8},{10,9},{11,10},{12... | collective-permute-start | bytes 1572872 | tf_op jit(solution)/shard_map/while/body/eval_jaxpr/ppermute | solution.py:28
  423.6 40.1 %collective-permute-start.1 = (f32[1,2,256,256]{3,2,1,0:T(8,128)S(1)}, f32[1,2,256,256]{3,2,1,0:T(8,128)S(1)}, u32[]{:S(2)}, u32[]{:S(2)}) collective-permute-start(f32[1,2,256,256]{3,2,1,0:T(8,128)S(1)} %get-tuple-element.1532), channel_id=1, source_target_pairs={{1,0},{2,1},{3,2},{4,3},{5,4},{6,5},{7,6},{9,8},{10,9},{11,10},{12... | collective-permute-start | bytes 1572872 | tf_op jit(solution)/shard_map/while/body/eval_jaxpr/ppermute | solution.py:28
  464.0 234.9 %collective-permute-start.1 = (f32[1,2,256,256]{3,2,1,0:T(8,128)S(1)}, f32[1,2,256,256]{3,2,1,0:T(8,128)S(1)}, u32[]{:S(2)}, u32[]{:S(2)}) collective-permute-start(f32[1,2,256,256]{3,2,1,0:T(8,128)S(1)} %get-tuple-element.1532), channel_id=1, source_target_pairs={{1,0},{2,1},{3,2},{4,3},{5,4},{6,5},{7,6},{9,8},{10,9},{11,10},{12... | collective-permute-start | bytes 1572872 | tf_op jit(solution)/shard_map/while/body/eval_jaxpr/ppermute | solution.py:28
  730.8 12.6 %collective-permute-start.1 = (f32[1,2,256,256]{3,2,1,0:T(8,128)S(1)}, f32[1,2,256,256]{3,2,1,0:T(8,128)S(1)}, u32[]{:S(2)}, u32[]{:S(2)}) collective-permute-start(f32[1,2,256,256]{3,2,1,0:T(8,128)S(1)} %get-tuple-element.1532), channel_id=1, source_target_pairs={{1,0},{2,1},{3,2},{4,3},{5,4},{6,5},{7,6},{9,8},{10,9},{11,10},{12... | collective-permute-start | bytes 1572872 | tf_op jit(solution)/shard_map/while/body/eval_jaxpr/ppermute | solution.py:28
  751.5 27.0 %collective-permute-start.4 = (f32[2,128,1024]{2,1,0:T(8,128)S(1)}, f32[2,128,1024]{2,1,0:T(8,128)S(1)}, u32[]{:S(2)}, u32[]{:S(2)}) collective-permute-start(f32[2,128,1024]{2,1,0:T(8,128)S(1)} %get-tuple-element.1402), channel_id=1, source_target_pairs={{0,248},{8,0},{16,8},{24,16},{32,24},{40,32},{48,40},{56,48},{64,5... | collective-permute-start | bytes 3145736 | tf_op jit(solution)/shard_map/ppermute | solution.py:34
  754.2 24.4 %collective-permute-start.5 = (f32[2,128,1024]{2,1,0:T(8,128)S(1)}, f32[2,128,1024]{2,1,0:T(8,128)S(1)}, u32[]{:S(2)}, u32[]{:S(2)}) collective-permute-start(f32[2,128,1024]{2,1,0:T(8,128)S(1)} %get-tuple-element.1403), channel_id=1, source_target_pairs={{0,8},{8,16},{16,24},{24,32},{32,40},{40,48},{48,56},{56,64},{64,7... | collective-permute-start | bytes 3145736 | tf_op jit(solution)/shard_map/ppermute | solution.py:34
where the time goes:
time: 783 us; the launch traced here: 780 us
  waiting for transfers between devices  510 us (65%)
  starting transfers between devices  155 us (20%)
  matrix products  48 us (6%)
  loops' own time  24.6 us (3%)
  other arithmetic  22.2 us (3%)
  local copies, waits for them, and re-layouts  15.2 us (2%)
    ppermute x16, waiting for transfers between devices, shifted(): return lax.ppermute(shard, axis, pairs)  466 us
    ppermute x16, starting transfers between devices, shifted(): return lax.ppermute(shard, axis, pairs)  147 us
    dot_general x32, matrix products, right_product(): return jnp.einsum('...jk,kl->...jl', field, matrix, precision=highest)  24.1 us
    dot_general x32, matrix products, left_product(): return jnp.einsum('jk,...kl->...jl', matrix, field, precision=highest)  23.9 us
    ppermute x2, waiting for transfers between devices, passed_along(): return lax.ppermute(value, axis, pairs)  23.7 us
    ppermute x1, waiting for transfers between devices, extended_2(): lax.ppermute(lax.slice_in_dim(block, block.shape[dim] - width, None, axis...  16.5 us
  transfers between devices with their start and end apart: 20, of which 19 were waited for; matrix products, arithmetic and copies ran while one was open for 0% of the time, Pallas kernels for 0%

commit v1 on v0

v1 whole, which is shorter than its diff:
```python
import jax
import jax.numpy as jnp
import ml_dtypes
import numpy as np
from jax import lax
from jax.experimental import pallas as pl
from jax.experimental.pallas import tpu as pltpu
from jax.sharding import PartitionSpec as P
W=256; HB=128
f32=jnp.float32; bf16=jnp.bfloat16

def fit(fn, degree, top):
    n=64
    z=(np.cos(np.pi*(np.arange(n)+.5)/n)+1)*top/2
    return np.polynomial.chebyshev.Chebyshev.fit(z, fn(z), degree, domain=[0,top]).convert(kind=np.polynomial.Polynomial).coef
SINC=fit(lambda z: np.sin(np.sqrt(z))/np.sqrt(z),6,9.0)
COSC=fit(lambda z: np.cos(np.sqrt(z)),6,9.0)

def halves(a):
    hi=a.astype(np.float32).astype(ml_dtypes.bfloat16)
    lo=(a-hi.astype(np.float64)).astype(np.float32).astype(ml_dtypes.bfloat16)
    return hi,lo

def tables():
    k=np.arange(W)
    F=np.exp(-2j*np.pi*((k[:,None]*k[None,:])%W)/W)/np.sqrt(W)
    fr=(((k+W//2)%W)-W//2)/W
    h=np.exp(-60j*fr*fr)
    A=np.conj(F)@np.diag(h)@F
    order=np.concatenate([np.arange(HB), W-1-np.arange(HB)])
    PP=A[:HB,:HB]; Q=A[:HB][:,order[HB:]]
    out=[]
    for B in ((PP+Q)/2,(PP-Q)/2):
        right=np.block([[B.real,B.imag],[-B.imag,B.real]])
        left=np.block([[B.real,-B.imag],[B.imag,B.real]])
        out.append((right,left))
    prop=[out[0][0],out[1][0],out[0][1],out[1][1]]
    G=F[:,order]
    far=[G.T.real,G.T.imag,G.real,G.imag]
    hp,lp=zip(*[halves(a) for a in prop]); hf,lf=zip(*[halves(a) for a in far])
    return np.stack([np.stack(hp),np.stack(lp)]), np.stack([np.stack(hf),np.stack(lf)])

def split(x):
    hi=x.astype(bf16)
    return hi,(x-hi.astype(f32)).astype(bf16)

def dot(a,b):
    return lax.dot_general(a,b,(((1,),(0,)),((),())),preferred_element_type=f32)

def mm_right(x, wh, wl):
    h,l=split(x)
    return dot(h,wh)+dot(l,wh)+dot(h,wl)
def mm_left(wh,wl,x):
    h,l=split(x)
    return dot(wh,h)+dot(wh,l)+dot(wl,h)

def propagate(ur,ui,T):
    ure,uro=ur[:,:HB]+ur[:,HB:],ur[:,:HB]-ur[:,HB:]
    uie,uio=ui[:,:HB]+ui[:,HB:],ui[:,:HB]-ui[:,HB:]
    ye=mm_right(jnp.concatenate([ure,uie],1),T[0,0],T[1,0])
    yo=mm_right(jnp.concatenate([uro,uio],1),T[0,1],T[1,1])
    te,be=ye[:HB]+ye[HB:],ye[:HB]-ye[HB:]
    to,bo=yo[:HB]+yo[HB:],yo[:HB]-yo[HB:]
    re=jnp.concatenate([jnp.concatenate([te[:,:HB],to[:,:HB]],1),jnp.concatenate([te[:,HB:],to[:,HB:]],1)],0)
    ro=jnp.concatenate([jnp.concatenate([be[:,:HB],bo[:,:HB]],1),jnp.concatenate([be[:,HB:],bo[:,HB:]],1)],0)
    ze=mm_left(T[0,2],T[1,2],re)
    zo=mm_left(T[0,3],T[1,3],ro)
    top=ze+zo; bot=ze-zo
    def unfold(t,b):
        return jnp.concatenate([jnp.concatenate([t[:,:HB]+t[:,HB:],t[:,:HB]-t[:,HB:]],1),
                                jnp.concatenate([b[:,:HB]+b[:,HB:],b[:,:HB]-b[:,HB:]],1)],0)
    return unfold(top[:HB],bot[:HB]),unfold(top[HB:],bot[HB:])

def cmm_right(xr,xi,rh,rl,ih,il):
    hr,lr=split(xr); hi,li=split(xi)
    yr=dot(hr,rh)+dot(lr,rh)+dot(hr,rl)-(dot(hi,ih)+dot(li,ih)+dot(hi,il))
    yi=dot(hr,ih)+dot(lr,ih)+dot(hr,il)+(dot(hi,rh)+dot(li,rh)+dot(hi,rl))
    return yr,yi
def cmm_left(rh,rl,ih,il,xr,xi):
    hr,lr=split(xr); hi,li=split(xi)
    yr=dot(rh,hr)+dot(rh,lr)+dot(rl,hr)-(dot(ih,hi)+dot(ih,li)+dot(il,hi))
    yi=dot(ih,hr)+dot(ih,lr)+dot(il,hr)+(dot(rh,hi)+dot(rh,li)+dot(rl,hi))
    return yr,yi

def poly(c,z):
    r=jnp.full_like(z,float(c[-1]))
    for a in c[-2::-1]:
        r=r*z+float(a)
    return r
def sincos(v):
    x=0.5*v; z=x*x
    return poly(COSC,z), x*poly(SINC,z)

def detector(ur,ui,inten,Fr):
    yr,yi=cmm_right(ur,ui,Fr[0,0],Fr[1,0],Fr[0,1],Fr[1,1])
    fr,fi=cmm_left(Fr[0,2],Fr[1,2],Fr[0,3],Fr[1,3],yr,yi)
    m=fr*fr+fi*fi-inten
    gr,gi=m*fr,-(m*fi)
    yr,yi=cmm_right(gr,gi,Fr[0,2],Fr[1,2],Fr[0,3],Fr[1,3])
    return cmm_left(Fr[0,0],Fr[1,0],Fr[0,1],Fr[1,1],yr,yi)

def chain_kernel(v_ref, p_ref, i_ref, T, Fr, d_ref, cs, us, ps):
    S=v_ref.shape[0]
    def load_t(s,_):
        c,n=sincos(v_ref[s])
        cs[s,0]=c; cs[s,1]=n
        return _
    lax.fori_loop(0,S,load_t,0)
    def trans(s,ar,ai):
        c,n=cs[s,0],cs[s,1]
        return c*ar-n*ai, c*ai+n*ar
    ps[0]=p_ref[0]; ps[1]=p_ref[1]
    def fwd(s,_):
        ur,ui=trans(s,ps[0],ps[1])
        us[s,0]=ur; us[s,1]=ui
        ps[0],ps[1]=propagate(ur,ui,T)
        return _
    lax.fori_loop(0,S-1,fwd,0)
    ur,ui=trans(S-1,ps[0],ps[1])
    us[S-1,0]=ur; us[S-1,1]=ui
    qr,qi=detector(ur,ui,i_ref[...],Fr)
    ps[0]=qr; ps[1]=qi
    d_ref[S-1]=-0.5*(qr*ui+qi*ur)
    def bwd(t,_):
        s=S-2-t
        gr,gi=trans(s+1,ps[0],ps[1])
        qr,qi=propagate(gr,gi,T)
        ps[0]=qr; ps[1]=qi
        d_ref[s]=-0.5*(qr*us[s,1]+qi*us[s,0])
        return _
    lax.fori_loop(0,S-1,bwd,0)

def chain(v,p,i,T,Fr):
    S=v.shape[0]
    vm=pl.BlockSpec(memory_space=pltpu.VMEM)
    return pl.pallas_call(chain_kernel,out_shape=jax.ShapeDtypeStruct((S,W,W),f32),
      in_specs=[vm]*5,out_specs=vm,
      scratch_shapes=[pltpu.VMEM((S,2,W,W),f32),pltpu.VMEM((S,2,W,W),f32),pltpu.VMEM((2,W,W),f32)],
      compiler_params=pltpu.CompilerParams(vmem_limit_bytes=56<<20))(v,p,i,T,Fr)


def exact_parts(x):
    high = lax.reduce_precision(x, 8, 7)
    rest = x - high
    mid = lax.reduce_precision(rest, 8, 7)
    return high.astype(bf16), mid.astype(bf16), (rest - mid).astype(bf16)


def select_right(x, chosen):
    a, b, c = exact_parts(x)
    return dot(a, chosen) + dot(b, chosen) + dot(c, chosen)


def select_left(chosen, x):
    a, b, c = exact_parts(x)
    return dot(chosen, a) + dot(chosen, b) + dot(chosen, c)


def fold(x, dim):
    low, high = jnp.split(x, 2, axis=dim)
    return jnp.concatenate([low, jnp.flip(high, dim)], axis=dim)


def folded(index):
    return jnp.where(index < HB, index, W + HB - 1 - index)


def local(potential, probe, positions, intensity):
    layers, strip, columns = potential.shape
    group = lax.axis_index("probe")
    groups = lax.axis_size("probe")
    depth = lax.axis_index("depth")
    up = [(i, (i + 1) % groups) for i in range(groups)]
    down = [(b, a) for a, b in up]
    mine = positions[0]
    before = lax.ppermute(mine, "probe", up)
    after = lax.ppermute(mine, "probe", down)
    place = folded(jnp.arange(W, dtype=jnp.int32))

    def column_pick(position):
        line = jnp.arange(columns, dtype=jnp.int32)[:, None]
        return (line == position[1] + place[None, :]).astype(bf16)

    own_pick, before_pick, after_pick = (column_pick(p) for p in (mine, before, after))
    flat = potential.reshape(layers * strip, columns)
    own = select_right(flat, own_pick).reshape(layers, strip, W)
    to_before = select_right(flat, before_pick).reshape(layers, strip, W)
    to_after = select_right(flat, after_pick).reshape(layers, strip, W)
    from_before = lax.ppermute(to_after, "probe", up)
    from_after = lax.ppermute(to_before, "probe", down)
    offset = (mine[0] - (group - 1) * strip) % (strip * groups)
    lines = jnp.arange(3 * strip, dtype=jnp.int32)
    row_pick = (lines[None, :] == offset + place[:, None]).astype(bf16)
    tall = jnp.concatenate([from_before, own, from_after], axis=1)
    windows = jnp.stack([select_left(row_pick, tall[s]) for s in range(layers)])
    every = lax.all_gather(windows, "depth", axis=0, tiled=True)
    T, Fr = tables()
    entry = fold(fold(probe, 1), 2)
    grads = chain(every, entry, intensity[0], jnp.asarray(T), jnp.asarray(Fr))
    grads = lax.dynamic_slice_in_dim(grads, depth * layers, layers, 0)
    tall = jnp.stack([select_left(row_pick.T, grads[s]) for s in range(layers)])
    from_after = lax.ppermute(tall[:, :strip], "probe", down)
    from_before = lax.ppermute(tall[:, 2 * strip :], "probe", up)

    def spread(x, pick):
        return select_right(x.reshape(layers * strip, W), pick.T).reshape(layers, strip, columns)

    return (
        spread(tall[:, strip : 2 * strip], own_pick)
        + spread(from_before, before_pick)
        + spread(from_after, after_pick)
    )


def solution(mesh):
    in_specs = (P("depth", "probe", None), P(), P("probe", None), P("probe", None, None))
    out_specs = P("depth", "probe", None)
    return jax.shard_map(local, mesh=mesh, in_specs=in_specs, out_specs=out_specs, check_vma=False)
```

time: 783 us -> 196 us (0.25)
  waiting for transfers between devices: 510 us -> 106 us
  starting transfers between devices: 155 us -> 12.9 us
  Pallas kernels: 0 us -> 35.7 us
  matrix products: 48 us -> 17.4 us
  loops' own time: 24.6 us -> 0 us
  other arithmetic: 22.2 us -> 5.52 us
  local copies, waits for them, and re-layouts: 15.2 us -> 3.02 us
  between operations: 4.89 us -> 14.3 us
    ppermute x20 -> x6, waiting for transfers between devices: 510 us -> 10.1 us  [the longest x1 5.07 us: local(): from_after = lax.ppermute(tall[:, :strip], 'probe', down)]
    ppermute x20 -> x6, starting transfers between devices: 155 us -> 12.9 us  [the longest x1 4.89 us: local(): from_after = lax.ppermute(to_before, 'probe', down)]
    all_gather x0 -> x1, waiting for transfers between devices: none -> 96.2 us  [local(): every = lax.all_gather(windows, 'depth', axis=0, tiled=True)]
    pallas_call x0 -> x1, Pallas kernels: none -> 35.7 us  [chain(): pl.pallas_call(chain_kernel, out_shape=jax.ShapeDtypeStruct((S, W, W), f3...]
    dot_general x64 -> x30, matrix products: 48 us -> 17.4 us  [dot(): lax.dot_general(a, b, (((1,), (0,)), ((), ())), preferred_element_type=f32)]
    another operation x19 -> x0, loops' own time: 24.6 us -> none  [the longest x1 15.4 us: local(): lax.fori_loop(0, blocks + depth_count - 1, backward_step, (empty_wave, gr...]
  transfers between devices with their start and end apart: 20 -> 7, of which waited for: 19 -> 4; matrix products, arithmetic and copies ran while one was open for 0% -> 6% of each run, Pallas kernels for 0% -> 0%
where the time goes in v1:
time: 196 us; the launch traced here: 195 us
  waiting for transfers between devices  106 us (54%)
  Pallas kernels  35.7 us (18%)
  matrix products  17.4 us (9%)
  between operations  14.3 us (7%)
  starting transfers between devices  12.9 us (7%)
  other arithmetic  5.52 us (3%)
  local copies, waits for them, and re-layouts  3.02 us (2%)
    all_gather x1, waiting for transfers between devices, local(): every = lax.all_gather(windows, 'depth', axis=0, tiled=True)  96.2 us
    pallas_call x1, Pallas kernels, chain(): pl.pallas_call(chain_kernel, out_shape=jax.ShapeDtypeStruct((S, W, W), f3...  35.7 us
    dot_general x30, matrix products, dot(): lax.dot_general(a, b, (((1,), (0,)), ((), ())), preferred_element_type=f32)  17.4 us
    ppermute x1, waiting for transfers between devices, local(): from_after = lax.ppermute(tall[:, :strip], 'probe', down)  5.07 us
    ppermute x1, starting transfers between devices, local(): from_after = lax.ppermute(to_before, 'probe', down)  4.89 us
  transfers between devices with their start and end apart: 7, of which 4 were waited for; matrix products, arithmetic and copies ran while one was open for 6% of the time, Pallas kernels for 0%

profile of v1, /device:TPU:1, one launch (start us, length us, event | category | flops | bytes accessed | tf_op | source)
XLA Modules:
  0.0 195.2 jit_solution(7927025523173724399)
XLA Ops:
  6.5 3.2 %collective-permute-start = (s32[2]{0:T(128)}, s32[2]{0:T(128)S(1)}, u32[]{:S(2)}, u32[]{:S(2)}) collective-permute-start(s32[2]{0:T(128)} %bitcast.124), channel_id=1, source_target_pairs={{8,0},{16,8},{24,16},{32,24},{40,32},{48,40},{56,48},{64,56},{72,6... | collective-permute-start | bytes 32 | tf_op jit(solution)/shard_map/ppermute | solution.py:177
  9.8 0.9 collective-permute-start.2
  10.7 1.3 fusion.70
  12.5 1.5 fusion.8
  14.1 0.7 broadcast_add_fusion.1
  15.5 0.6 slice.36
  16.1 0.6 broadcast_add_fusion.2
  17.9 0.6 collective-permute-start.1
  18.5 0.6 slice.38
  19.1 0.6 broadcast_add_fusion
  20.9 4.9 %collective-permute-start.3 = (f32[2,128,256]{2,1,0:T(8,128)S(1)}, f32[2,128,256]{2,1,0:T(8,128)S(1)}, u32[]{:S(2)}, u32[]{:S(2)}) collective-permute-start(f32[2,128,256]{2,1,0:T(8,128)S(1)} %bitcast.127), channel_id=1, source_target_pairs={{8,0},{16,8},{24,16},{32,24},{40,32},{48,40},{56,48},{64,56},{72,6... | collective-permute-start | bytes 786440 | tf_op jit(solution)/shard_map/ppermute | solution.py:190
  26.2 2.5 %collective-permute-done.3 = f32[2,128,256]{2,1,0:T(8,128)S(1)} collective-permute-done((f32[2,128,256]{2,1,0:T(8,128)S(1)}, f32[2,128,256]{2,1,0:T(8,128)S(1)}, u32[]{:S(2)}, u32[]{:S(2)}) %collective-permute-start.3) | collective-permute-done | bytes 262176 | tf_op jit(solution)/shard_map/ppermute | solution.py:190
  30.5 0.8 pad_maximum_fusion.1
  31.9 0.9 pad_maximum_fusion.2.p_ref
  32.8 96.2 %all-gather.2.cloned.1.call-done.v_ref = f32[16,256,256]{2,1,0:T(8,128)} async-done(((f32[2,256,256]{2,1,0:T(8,128)}), f32[16,256,256]{2,1,0:T(8,128)}) %all-gather.2.cloned.1.call-update) | async-done | bytes 4194320 | tf_op jit(solution)/shard_map/all_gather | solution.py:196
  129.1 35.7 %shard_map.64 = f32[16,256,256]{2,1,0:T(8,128)} custom-call(f32[16,256,256]{2,1,0:T(8,128)} %all-gather.2.cloned.1.call-done.v_ref, f32[2,256,256]{2,1,0:T(8,128)} %pad_maximum_fusion.2.p_ref, f32[256,256]{1,0:T(8,128)} %bitcast.122, bf16[2,4,256,256]{3,2,1,0:T(8,128)(2,1)} %constant.39.clone.T, bf16[2,4,256,256]{3,2,1,0:T(8,128)(2,1)} %constant.40.clone.Fr), custom_call_target="tpu_custom_call" | custom-call | tf_op jit(solution)/shard_map/pallas_call | solution.py:136
  164.7 1.3 fusion.35
  166.0 1.3 convolution_add_fusion.7
  167.4 1.3 fusion.5
  168.7 1.3 fusion.34
  170.0 1.3 convolution_add_fusion.5
  171.3 1.3 fusion.4
  172.8 0.4 fusion.11
  173.2 3.3 %collective-permute-start.4 = (f32[2,128,256]{2,1,0:T(8,128)S(1)}, f32[2,128,256]{2,1,0:T(8,128)S(1)}, u32[]{:S(2)}, u32[]{:S(2)}) collective-permute-start(f32[2,128,256]{2,1,0:T(8,128)S(1)} %get-tuple-element.10), channel_id=1, source_target_pairs={{0,8},{8,16},{16,24},{24,32},{32,40},{40,48},{48,56},{56,64},{64,7... | collective-permute-start | bytes 786440 | tf_op jit(solution)/shard_map/ppermute | solution.py:203
  176.5 0.4 convolution_add_fusion.3
  176.9 0.4 convolution_add_fusion.2
  177.3 2.5 %collective-permute-done.4 = f32[2,128,256]{2,1,0:T(8,128)S(1)} collective-permute-done((f32[2,128,256]{2,1,0:T(8,128)S(1)}, f32[2,128,256]{2,1,0:T(8,128)S(1)}, u32[]{:S(2)}, u32[]{:S(2)}) %collective-permute-start.4) | collective-permute-done | bytes 262176 | tf_op jit(solution)/shard_map/ppermute | solution.py:203
  179.8 0.4 fusion.10
  180.6 5.1 %collective-permute-done.5 = f32[2,128,256]{2,1,0:T(8,128)S(1)} collective-permute-done((f32[2,128,256]{2,1,0:T(8,128)S(1)}, f32[2,128,256]{2,1,0:T(8,128)S(1)}, u32[]{:S(2)}, u32[]{:S(2)}) %collective-permute-start.5) | collective-permute-done | bytes 262176 | tf_op jit(solution)/shard_map/ppermute | solution.py:202
  186.2 0.4 fusion.13
  186.6 0.4 fusion.3
  187.0 1.4 fusion.1
  (35 shorter events, 6.7 us)
Async XLA Ops:
  6.5 122.5 %all-gather.2.cloned.1.call-start = ((), (), s32[]{:S(2)}) async-start(), calls=%async_computation | async-start | bytes 4718592 | tf_op jit(solution)/shard_map/all_gather | solution.py:196
  6.5 9.0 %collective-permute-start = (s32[2]{0:T(128)}, s32[2]{0:T(128)S(1)}, u32[]{:S(2)}, u32[]{:S(2)}) collective-permute-start(s32[2]{0:T(128)} %bitcast.124), channel_id=1, source_target_pairs={{8,0},{16,8},{24,16},{32,24},{40,32},{48,40},{56,48},{64,56},{72,6... | collective-permute-start | bytes 32 | tf_op jit(solution)/shard_map/ppermute | solution.py:177
  9.8 8.7 %collective-permute-start.2 = (s32[2]{0:T(128)}, s32[2]{0:T(128)S(1)}, u32[]{:S(2)}, u32[]{:S(2)}) collective-permute-start(s32[2]{0:T(128)} %bitcast.125), channel_id=1, source_target_pairs={{0,8},{8,16},{16,24},{24,32},{32,40},{40,48},{48,56},{56,64},{64,7... | collective-permute-start | bytes 32 | tf_op jit(solution)/shard_map/ppermute | solution.py:176
  17.9 8.3 %collective-permute-start.1 = (f32[2,128,256]{2,1,0:T(8,128)S(1)}, f32[2,128,256]{2,1,0:T(8,128)S(1)}, u32[]{:S(2)}, u32[]{:S(2)}) collective-permute-start(f32[2,128,256]{2,1,0:T(8,128)S(1)} %bitcast.126), channel_id=1, source_target_pairs={{0,8},{8,16},{16,24},{24,32},{32,40},{40,48},{48,56},{56,64},{64,7... | collective-permute-start | bytes 786440 | tf_op jit(solution)/shard_map/ppermute | solution.py:189
  20.9 7.8 %collective-permute-start.3 = (f32[2,128,256]{2,1,0:T(8,128)S(1)}, f32[2,128,256]{2,1,0:T(8,128)S(1)}, u32[]{:S(2)}, u32[]{:S(2)}) collective-permute-start(f32[2,128,256]{2,1,0:T(8,128)S(1)} %bitcast.127), channel_id=1, source_target_pairs={{8,0},{16,8},{24,16},{32,24},{40,32},{48,40},{56,48},{64,56},{72,6... | collective-permute-start | bytes 786440 | tf_op jit(solution)/shard_map/ppermute | solution.py:190
  26.2 5.1 %copy-start = (f32[2,256,256]{2,1,0:T(8,128)S(1)}, f32[2,256,256]{2,1,0:T(8,128)}, u32[]{:S(2)}) copy-start(f32[2,256,256]{2,1,0:T(8,128)} %param.7) | copy-start | bytes 1572868
  173.2 6.6 %collective-permute-start.4 = (f32[2,128,256]{2,1,0:T(8,128)S(1)}, f32[2,128,256]{2,1,0:T(8,128)S(1)}, u32[]{:S(2)}, u32[]{:S(2)}) collective-permute-start(f32[2,128,256]{2,1,0:T(8,128)S(1)} %get-tuple-element.10), channel_id=1, source_target_pairs={{0,8},{8,16},{16,24},{24,32},{32,40},{40,48},{48,56},{56,64},{64,7... | collective-permute-start | bytes 786440 | tf_op jit(solution)/shard_map/ppermute | solution.py:203
  176.5 9.2 %collective-permute-start.5 = (f32[2,128,256]{2,1,0:T(8,128)S(1)}, f32[2,128,256]{2,1,0:T(8,128)S(1)}, u32[]{:S(2)}, u32[]{:S(2)}) collective-permute-start(f32[2,128,256]{2,1,0:T(8,128)S(1)} %get-tuple-element.8), channel_id=1, source_target_pairs={{8,0},{16,8},{24,16},{32,24},{40,32},{48,40},{56,48},{64,56},{72,6... | collective-permute-start | bytes 786440 | tf_op jit(solution)/shard_map/ppermute | solution.py:202
Sparse Core Ops, SparseCore 0:
  31.4 97.5 all-gather.1

commit v2 on v1

v2 whole, which is shorter than its diff:
```python
import functools

import jax
import jax.numpy as jnp
import ml_dtypes
import numpy as np
from jax import lax
from jax.experimental import pallas as pl
from jax.experimental.pallas import tpu as pltpu
from jax.sharding import PartitionSpec as P
W=256; HB=128
f32=jnp.float32; bf16=jnp.bfloat16

def fit(fn, degree, top):
    n=64
    z=(np.cos(np.pi*(np.arange(n)+.5)/n)+1)*top/2
    return np.polynomial.chebyshev.Chebyshev.fit(z, fn(z), degree, domain=[0,top]).convert(kind=np.polynomial.Polynomial).coef
SINC=fit(lambda z: np.sin(np.sqrt(z))/np.sqrt(z),6,9.0)
COSC=fit(lambda z: np.cos(np.sqrt(z)),6,9.0)

def halves(a):
    hi=a.astype(np.float32).astype(ml_dtypes.bfloat16)
    lo=(a-hi.astype(np.float64)).astype(np.float32).astype(ml_dtypes.bfloat16)
    return hi,lo

def tables():
    k=np.arange(W)
    F=np.exp(-2j*np.pi*((k[:,None]*k[None,:])%W)/W)/np.sqrt(W)
    fr=(((k+W//2)%W)-W//2)/W
    h=np.exp(-60j*fr*fr)
    A=np.conj(F)@np.diag(h)@F
    order=np.concatenate([np.arange(HB), W-1-np.arange(HB)])
    PP=A[:HB,:HB]; Q=A[:HB][:,order[HB:]]
    out=[]
    for B in ((PP+Q)/2,(PP-Q)/2):
        right=np.block([[B.real,B.imag],[-B.imag,B.real]])
        left=np.block([[B.real,-B.imag],[B.imag,B.real]])
        out.append((right,left))
    prop=[out[0][0],out[1][0],out[0][1],out[1][1]]
    G=F[:,order]
    far=[G.T.real,G.T.imag,G.real,G.imag]
    hp,lp=zip(*[halves(a) for a in prop]); hf,lf=zip(*[halves(a) for a in far])
    return np.stack([np.stack(hp),np.stack(lp)]), np.stack([np.stack(hf),np.stack(lf)])

def split(x):
    hi=x.astype(bf16)
    return hi,(x-hi.astype(f32)).astype(bf16)

def dot(a,b):
    return lax.dot_general(a,b,(((1,),(0,)),((),())),preferred_element_type=f32)

def mm_right(x, wh, wl):
    h,l=split(x)
    return dot(h,wh)+dot(l,wh)+dot(h,wl)
def mm_left(wh,wl,x):
    h,l=split(x)
    return dot(wh,h)+dot(wh,l)+dot(wl,h)

def propagate(ur,ui,T):
    ure,uro=ur[:,:HB]+ur[:,HB:],ur[:,:HB]-ur[:,HB:]
    uie,uio=ui[:,:HB]+ui[:,HB:],ui[:,:HB]-ui[:,HB:]
    ye=mm_right(jnp.concatenate([ure,uie],1),T[0,0],T[1,0])
    yo=mm_right(jnp.concatenate([uro,uio],1),T[0,1],T[1,1])
    te,be=ye[:HB]+ye[HB:],ye[:HB]-ye[HB:]
    to,bo=yo[:HB]+yo[HB:],yo[:HB]-yo[HB:]
    re=jnp.concatenate([jnp.concatenate([te[:,:HB],to[:,:HB]],1),jnp.concatenate([te[:,HB:],to[:,HB:]],1)],0)
    ro=jnp.concatenate([jnp.concatenate([be[:,:HB],bo[:,:HB]],1),jnp.concatenate([be[:,HB:],bo[:,HB:]],1)],0)
    ze=mm_left(T[0,2],T[1,2],re)
    zo=mm_left(T[0,3],T[1,3],ro)
    top=ze+zo; bot=ze-zo
    def unfold(t,b):
        return jnp.concatenate([jnp.concatenate([t[:,:HB]+t[:,HB:],t[:,:HB]-t[:,HB:]],1),
                                jnp.concatenate([b[:,:HB]+b[:,HB:],b[:,:HB]-b[:,HB:]],1)],0)
    return unfold(top[:HB],bot[:HB]),unfold(top[HB:],bot[HB:])

def cmm_right(xr,xi,rh,rl,ih,il):
    hr,lr=split(xr); hi,li=split(xi)
    yr=dot(hr,rh)+dot(lr,rh)+dot(hr,rl)-(dot(hi,ih)+dot(li,ih)+dot(hi,il))
    yi=dot(hr,ih)+dot(lr,ih)+dot(hr,il)+(dot(hi,rh)+dot(li,rh)+dot(hi,rl))
    return yr,yi
def cmm_left(rh,rl,ih,il,xr,xi):
    hr,lr=split(xr); hi,li=split(xi)
    yr=dot(rh,hr)+dot(rh,lr)+dot(rl,hr)-(dot(ih,hi)+dot(ih,li)+dot(il,hi))
    yi=dot(ih,hr)+dot(ih,lr)+dot(il,hr)+(dot(rh,hi)+dot(rh,li)+dot(rl,hi))
    return yr,yi

def poly(c,z):
    r=jnp.full_like(z,float(c[-1]))
    for a in c[-2::-1]:
        r=r*z+float(a)
    return r
def sincos(v):
    x=0.5*v; z=x*x
    return poly(COSC,z), x*poly(SINC,z)

def detector(ur,ui,inten,Fr):
    yr,yi=cmm_right(ur,ui,Fr[0,0],Fr[1,0],Fr[0,1],Fr[1,1])
    fr,fi=cmm_left(Fr[0,2],Fr[1,2],Fr[0,3],Fr[1,3],yr,yi)
    m=fr*fr+fi*fi-inten
    gr,gi=m*fr,-(m*fi)
    yr,yi=cmm_right(gr,gi,Fr[0,2],Fr[1,2],Fr[0,3],Fr[1,3])
    return cmm_left(Fr[0,0],Fr[1,0],Fr[0,1],Fr[1,1],yr,yi)


def exact_parts(x):
    high = x.astype(bf16)
    rest = x - high.astype(f32)
    mid = rest.astype(bf16)
    return high, mid, (rest - mid.astype(f32)).astype(bf16)


def select_right(x, chosen):
    a, b, c = exact_parts(x)
    return dot(a, chosen) + dot(b, chosen) + dot(c, chosen)


def select_left(chosen, x):
    a, b, c = exact_parts(x)
    return dot(chosen, a) + dot(chosen, b) + dot(chosen, c)


def spread(x, chosen):
    return sum(
        lax.dot_general(part, chosen, (((1,), (1,)), ((), ())), preferred_element_type=f32)
        for part in exact_parts(x)
    )


def folded(shape, dim):
    index = lax.broadcasted_iota(jnp.int32, shape, dim)
    return jnp.where(index < HB, index, W + HB - 1 - index)


def ones_where(condition):
    return jnp.where(condition, 1.0, 0.0).astype(bf16)


def wide(row, width):
    return jnp.concatenate([row] * (width // 128), axis=1)


def kernel(
    groups, depths, v_ref, p_ref, pos_ref, i_ref, T, Fr, o_ref,
    V, cs, us, ps, dbuf, pos_out, pos_in, halo_out, halo_in, dep_out, dep_in, own_cut, pick,
    pos_ss, pos_rs, halo_ss, halo_rs, send_v, recv_v, relay_s, send_d, recv_d, dep_ss, dep_rs,
):
    layers, strip, columns = v_ref.shape
    slices = layers * depths
    rows = groups * strip
    g = lax.axis_index("probe")
    d = lax.axis_index("depth")
    y = d // 2
    xl = d % 2
    core = g % 2
    active = xl == core
    before, after = (g + groups - 1) % groups, (g + 1) % groups
    home = 2 * y + core
    partner = d + 1 - 2 * xl
    up, down = (home + 2) % depths, (home + depths - 2) % depths

    def there(probe_at, depth_at):
        return {"probe": probe_at, "depth": depth_at}

    barrier = pltpu.get_barrier_semaphore()
    peers = [there(before, d), there(after, d), there(g, partner)]
    for base in (d, partner):
        peers.append(there(g, (base + 2) % depths))
        peers.append(there(g, (base + depths - 2) % depths))
    for peer in peers:
        pl.semaphore_signal(barrier, inc=1, device_id=peer, device_id_type=pl.DeviceIdType.MESH)
    pos_out[0] = jnp.full((8, 128), pos_ref[0, 0], jnp.int32)
    pos_out[1] = jnp.full((8, 128), pos_ref[0, 1], jnp.int32)
    pl.semaphore_wait(barrier, len(peers))

    def remote(source, target, sent, received, where):
        return pltpu.make_async_remote_copy(
            src_ref=source, dst_ref=target, send_sem=sent, recv_sem=received,
            device_id=where, device_id_type=pl.DeviceIdType.MESH,
        )

    near = (there(before, d), there(after, d))
    pos_copy = [remote(pos_out, pos_in.at[1 - n], pos_ss.at[n], pos_rs.at[1 - n], near[n]) for n in (0, 1)]
    for n in (0, 1):
        pos_copy[n].start()

    lines = lax.broadcasted_iota(jnp.int32, (columns, W), 0)
    place = folded((columns, W), 1)

    def column_pick(left):
        return ones_where(lines == place + wide(left, W))

    pick[2] = column_pick(pos_out[1][:1])
    for s in range(layers):
        own_cut[s] = select_right(v_ref[s], pick[2])
    fold = ones_where(lax.broadcasted_iota(jnp.int32, (W, W), 0) == folded((W, W), 1))
    for c in (0, 1):
        ps[c] = select_left(fold, select_right(p_ref[c], fold))
    offset = (pos_out[0][:1] - (g - 1) * strip + rows) & (rows - 1)
    row_pick = ones_where(
        lax.broadcasted_iota(jnp.int32, (W, 3 * strip), 1) == folded((W, 3 * strip), 0) + wide(offset, 3 * strip)
    )
    row_back = ones_where(
        lax.broadcasted_iota(jnp.int32, (3 * strip, W), 0) == folded((3 * strip, W), 1) + wide(offset, W)
    )

    halo_copy = [
        [remote(halo_out.at[n, s], halo_in.at[1 - n, s], halo_ss.at[n, s], halo_rs.at[1 - n, s], near[n]) for s in range(layers)]
        for n in (0, 1)
    ]
    for n in (0, 1):
        pos_copy[1 - n].wait_recv()
        pick[n] = column_pick(pos_in[n, 1][:1])
    for s in range(layers):
        for n in (0, 1):
            halo_out[n, s] = select_right(v_ref[s], pick[n])
            halo_copy[n][s].start()

    def window_copy(slice_at, sent, depth_at):
        return remote(V.at[slice_at], V.at[slice_at], sent, recv_v.at[slice_at], there(g, depth_at))

    for s in range(layers):
        mine = layers * d + s
        halo_copy[1][s].wait_recv()
        halo_copy[0][s].wait_recv()
        tall = jnp.concatenate([halo_in[0, s], own_cut[s], halo_in[1, s]], axis=0)
        V[mine] = select_left(row_pick, tall)

        @pl.when(jnp.logical_not(active))
        def _():
            window_copy(mine, send_v.at[2, s], partner).start()

        window_copy(mine, send_v.at[0, s], up).start()
        window_copy(mine, send_v.at[1, s], down).start()

    per = 2 * layers

    def gradient_copy(slot):
        return remote(dbuf.at[slot], dbuf.at[slot], send_d.at[slot % 2], recv_d.at[slot % 2], there(g, partner))

    def trans(s, ar, ai):
        c, n = cs[s, 0], cs[s, 1]
        return c * ar - n * ai, c * ai + n * ar

    @pl.when(active)
    def _():
        low, high = (y + 3) % 4, (y + 1) % 4
        first, last = y == 1, y == 3
        steps = [(low * per + j, jnp.where(first, j, (2, 5)[j]), up) for j in (0, 1)]
        steps += [(high * per + j, jnp.where(last, j, (4, 7)[j - 2]), down) for j in (2, 3)]

        def arrive(s):
            for k, (which, when, where) in enumerate(steps):
                @pl.when(s == when)
                def _():
                    window_copy(which, relay_s.at[k], where).wait_recv()
                    window_copy(which, relay_s.at[k], where).start()

            passed_on = ((s // per == low) & (s % per < 2)) | ((s // per == high) & (s % per >= 2))

            @pl.when((s // layers != d) & jnp.logical_not(passed_on))
            def _():
                window_copy(s, relay_s.at[0], partner).wait_recv()

        def enter(s):
            c, n = sincos(V[s])
            cs[s, 0] = c
            cs[s, 1] = n
            ar, ai = ps[0], ps[1]
            ur, ui = c * ar - n * ai, c * ai + n * ar

            @pl.when(s // per == y)
            def _():
                us[s % per, 0] = ur
                us[s % per, 1] = ui

            return ur, ui

        def leave(s, qr, qi):
            @pl.when(s // per == y)
            def _():
                slot = s % per
                dbuf[slot] = -0.5 * (qr * us[slot, 1] + qi * us[slot, 0])

                @pl.when(slot // layers != xl)
                def _():
                    gradient_copy(slot).start()

        @pl.loop(0, slices - 1)
        def _(s):
            arrive(s)
            ur, ui = enter(s)
            ps[0], ps[1] = propagate(ur, ui, T)

        arrive(slices - 1)
        ur, ui = enter(slices - 1)
        qr, qi = detector(ur, ui, i_ref[0], Fr)
        ps[0] = qr
        ps[1] = qi
        leave(slices - 1, qr, qi)

        @pl.loop(0, slices - 1 - per * y)
        def _(t):
            s = slices - 2 - t
            gr, gi = trans(s + 1, ps[0], ps[1])
            qr, qi = propagate(gr, gi, T)
            ps[0] = qr
            ps[1] = qi
            leave(s, qr, qi)

    dep_copy = [
        [remote(dep_out.at[n, s], dep_in.at[1 - n, s], dep_ss.at[n, s], dep_rs.at[1 - n, s], near[n]) for s in range(layers)]
        for n in (0, 1)
    ]
    for s in (1, 0):
        slot = layers * xl + s

        @pl.when(jnp.logical_not(active))
        def _():
            gradient_copy(slot).wait_recv()

        tall = select_left(row_back, dbuf[slot])
        dep_out[0, s] = tall[:strip]
        dep_copy[0][s].start()
        dep_out[1, s] = tall[2 * strip :]
        dep_copy[1][s].start()
        o_ref[s] = spread(tall[strip : 2 * strip], pick[2])
    for s in (1, 0):
        for n in (0, 1):
            dep_copy[1 - n][s].wait_recv()
            o_ref[s] += spread(dep_in[n, s], pick[n])

    for n in (0, 1):
        pos_copy[n].wait_send()
        for s in range(layers):
            halo_copy[n][s].wait_send()
            dep_copy[n][s].wait_send()
    for s in range(layers):
        mine = layers * d + s
        window_copy(mine, send_v.at[0, s], up).wait_send()
        window_copy(mine, send_v.at[1, s], down).wait_send()

    @pl.when(jnp.logical_not(active))
    def _():
        for s in range(layers):
            window_copy(layers * d + s, send_v.at[2, s], partner).wait_send()

    @pl.when(active)
    def _():
        for k in range(4):
            window_copy(0, relay_s.at[k], up).wait_send()
        for s in range(layers):
            gradient_copy(layers * (1 - xl) + s).wait_send()


def local(potential, probe, positions, intensity):
    layers, strip, columns = potential.shape
    groups = lax.axis_size("probe")
    depths = lax.axis_size("depth")
    slices = layers * depths
    T, Fr = tables()
    vm = pl.BlockSpec(memory_space=pltpu.VMEM)
    dma = pltpu.SemaphoreType.DMA
    return pl.pallas_call(
        functools.partial(kernel, groups, depths),
        out_shape=jax.ShapeDtypeStruct(potential.shape, f32),
        in_specs=[vm, vm, pl.BlockSpec(memory_space=pltpu.SMEM), vm, vm, vm],
        out_specs=vm,
        scratch_shapes=[
            pltpu.VMEM((slices, W, W), f32),
            pltpu.VMEM((slices, 2, W, W), f32),
            pltpu.VMEM((2 * layers, 2, W, W), f32),
            pltpu.VMEM((2, W, W), f32),
            pltpu.VMEM((2 * layers, W, W), f32),
            pltpu.VMEM((2, 8, 128), jnp.int32),
            pltpu.VMEM((2, 2, 8, 128), jnp.int32),
            pltpu.VMEM((2, layers, strip, W), f32),
            pltpu.VMEM((2, layers, strip, W), f32),
            pltpu.VMEM((2, layers, strip, W), f32),
            pltpu.VMEM((2, layers, strip, W), f32),
            pltpu.VMEM((layers, strip, W), f32),
            pltpu.VMEM((3, columns, W), bf16),
            dma((2,)), dma((2,)), dma((2, layers)), dma((2, layers)),
            dma((3, layers)), dma((slices,)), dma((4,)), dma((2,)), dma((2,)),
            dma((2, layers)), dma((2, layers)),
        ],
        compiler_params=pltpu.CompilerParams(
            collective_id=0, has_side_effects=True, vmem_limit_bytes=56 << 20
        ),
    )(potential, probe, positions, intensity, jnp.asarray(T), jnp.asarray(Fr))


def solution(mesh):
    in_specs = (P("depth", "probe", None), P(), P("probe", None), P("probe", None, None))
    out_specs = P("depth", "probe", None)
    return jax.shard_map(local, mesh=mesh, in_specs=in_specs, out_specs=out_specs, check_vma=False)
```

time: 196 us -> 97.7 us (0.50)
  the two profiles are of different devices: /device:TPU:1 before, /device:TPU:0 now
where the time goes in v2:
time: 97.7 us; the launch traced here: 97.5 us
  Pallas kernels  95.2 us (97%)
  local copies, waits for them, and re-layouts  2.31 us (2%)
    pallas_call x1, Pallas kernels, local(): pl.pallas_call(functools.partial(kernel, groups, depths), out_shape=jax.S...  95.2 us
    unnamed x1, local copies, waits for them, and re-layouts  2.31 us

profile of v2, /device:TPU:0, one launch (start us, length us, event | category | flops | bytes accessed | tf_op | source)
XLA Modules:
  0.0 97.5 jit_solution(14288698571239647196)
XLA Ops:
  0.0 95.2 %shard_map.64 = f32[2,128,1024]{2,1,0:T(8,128)} custom-call(f32[2,128,1024]{2,1,0:T(8,128)} %v_ref.1, f32[2,256,256]{2,1,0:T(8,128)} %p_ref.1, s32[1,2]{1,0:T(1,128)} %pos_ref.1, f32[1,256,256]{2,1,0:T(8,128)} %i_ref.1, bf16[2,4,256,256]{3,2,1,0:T(8,128)(2,1)} %constant.4.clone.T, bf16[2,4,256,256]{3,2,1,0:T(8,128)(2,1)} %constant.5.clone.Fr), custom_call_target="tpu_custom_call" | custom-call | tf_op jit(solution)/shard_map/pallas_call | solution.py:363
  95.2 2.3 %copy.8 = f32[2,128,1024]{2,1,0:T(8,128)} copy(f32[2,128,1024]{2,1,0:T(8,128)} %shard_map.64) | data formatting | bytes 2097152

commit v3 on v2

--- a/solution.py
+++ b/solution.py
@@ -141,8 +141,8 @@
 
 def kernel(
     groups, depths, v_ref, p_ref, pos_ref, i_ref, T, Fr, o_ref,
-    V, cs, us, ps, dbuf, pos_out, pos_in, halo_out, halo_in, dep_out, dep_in, own_cut, pick,
-    pos_ss, pos_rs, halo_ss, halo_rs, send_v, recv_v, relay_s, send_d, recv_d, dep_ss, dep_rs,
+    V, held, cs, us, ps, pos_out, pos_in, halo_out, halo_in, dep_out, dep_mid, dep_in, own_cut, pick,
+    pos_ss, pos_rs, halo_ss, halo_rs, send_v, recv_v, held_s, held_r, dep_ss, dep_rs, mid_s, mid_r,
 ):
     layers, strip, columns = v_ref.shape
     slices = layers * depths
@@ -154,18 +154,17 @@
     core = g % 2
     active = xl == core
     before, after = (g + groups - 1) % groups, (g + 1) % groups
-    home = 2 * y + core
+    beside = g + 1 - 2 * core
     partner = d + 1 - 2 * xl
-    up, down = (home + 2) % depths, (home + depths - 2) % depths
+    up, down = (d + 2) % depths, (d + depths - 2) % depths
 
     def there(probe_at, depth_at):
         return {"probe": probe_at, "depth": depth_at}
 
     barrier = pltpu.get_barrier_semaphore()
-    peers = [there(before, d), there(after, d), there(g, partner)]
-    for base in (d, partner):
-        peers.append(there(g, (base + 2) % depths))
-        peers.append(there(g, (base + depths - 2) % depths))
+    peers = [there(near_by, at) for near_by in (before, after) for at in (d, partner)]
+    peers += [there(g, partner)]
+    peers += [there(near_by, at) for near_by in (g, beside) for at in (up, down)]
     for peer in peers:
         pl.semaphore_signal(barrier, inc=1, device_id=peer, device_id_type=pl.DeviceIdType.MESH)
     pos_out[0] = jnp.full((8, 128), pos_ref[0, 0], jnp.int32)
@@ -215,8 +214,26 @@
             halo_out[n, s] = select_right(v_ref[s], pick[n])
             halo_copy[n][s].start()
 
-    def window_copy(slice_at, sent, depth_at):
-        return remote(V.at[slice_at], V.at[slice_at], sent, recv_v.at[slice_at], there(g, depth_at))
+    def into_window(source, slice_at, sent, probe_at, depth_at):
+        return remote(source, V.at[slice_at], sent, recv_v.at[slice_at], there(probe_at, depth_at))
+
+    def into_held(source, k, sent, probe_at, depth_at):
+        return remote(source, held.at[k], sent, held_r.at[k], there(probe_at, depth_at))
+
+    def own_sends(s):
+        mine = layers * d + s
+        if s == 0:
+            return (
+                into_held(V.at[mine], 2, send_v.at[s, 0], beside, up),
+                into_window(V.at[mine], mine, send_v.at[s, 1], g, down),
+            )
+        return (
+            into_window(V.at[mine], mine, send_v.at[s, 0], g, up),
+            into_held(V.at[mine], 4, send_v.at[s, 1], beside, down),
+        )
+
+    def other_send(s):
+        return into_held(V.at[layers * d + s], s, send_v.at[s, 0], beside, partner)
 
     for s in range(layers):
         mine = layers * d + s
@@ -225,17 +242,53 @@
         tall = jnp.concatenate([halo_in[0, s], own_cut[s], halo_in[1, s]], axis=0)
         V[mine] = select_left(row_pick, tall)
 
+        @pl.when(active)
+        def _():
+            for copy in own_sends(s):
+                copy.start()
+
         @pl.when(jnp.logical_not(active))
         def _():
-            window_copy(mine, send_v.at[2, s], partner).start()
-
-        window_copy(mine, send_v.at[0, s], up).start()
-        window_copy(mine, send_v.at[1, s], down).start()
+            other_send(s).start()
 
     per = 2 * layers
 
-    def gradient_copy(slot):
-        return remote(dbuf.at[slot], dbuf.at[slot], send_d.at[slot % 2], recv_d.at[slot % 2], there(g, partner))
+    def passing():
+        low, high = (partner + depths - 2) % depths, (partner + 2) % depths
+
+        def sends(k, slice_at, *targets):
+            out = [into_window(held.at[k], slice_at, held_s.at[k, 0], beside, d)]
+            for n, (what, where) in enumerate(targets):
+                if what is None:
+                    out.append(into_window(held.at[k], slice_at, held_s.at[k, n + 1], beside, where))
+                else:
+                    out.append(into_held(held.at[k], what, held_s.at[k, n + 1], g, where))
+            return k, out
+
+        return (
+            sends(0, layers * partner, (3, up), (None, down)),
+            sends(2, layers * down, (None, up)),
+            sends(4, layers * up + 1, (None, down)),
+            sends(1, layers * partner + 1, (None, up), (5, down)),
+            sends(3, layers * low, (None, up)),
+            sends(5, layers * high + 1, (None, down)),
+        )
+
+    @pl.when(jnp.logical_not(active))
+    def _():
+        for k, copies in passing():
+            into_held(held.at[k], k, held_s.at[k, 0], beside, d).wait_recv()
+            for copy in copies:
+                copy.start()
+
+    def edge_copy(n, slot):
+        return remote(
+            dep_out.at[n, slot], dep_in.at[1 - n, slot % layers], dep_ss.at[n, slot],
+            dep_rs.at[1 - n, slot % layers], there((before, after)[n], 2 * y + slot // layers),
+        )
+
+    def middle_copy(slot):
+        return remote(dep_mid.at[slot], dep_mid.at[slot], mid_s.at[slot % layers], mid_r.at[slot % layers], there(g, partner))
 
     def trans(s, ar, ai):
         c, n = cs[s, 0], cs[s, 1]
@@ -243,23 +296,10 @@
 
     @pl.when(active)
     def _():
-        low, high = (y + 3) % 4, (y + 1) % 4
-        first, last = y == 1, y == 3
-        steps = [(low * per + j, jnp.where(first, j, (2, 5)[j]), up) for j in (0, 1)]
-        steps += [(high * per + j, jnp.where(last, j, (4, 7)[j - 2]), down) for j in (2, 3)]
-
         def arrive(s):
-            for k, (which, when, where) in enumerate(steps):
-                @pl.when(s == when)
-                def _():
-                    window_copy(which, relay_s.at[k], where).wait_recv()
-                    window_copy(which, relay_s.at[k], where).start()
-
-            passed_on = ((s // per == low) & (s % per < 2)) | ((s // per == high) & (s % per >= 2))
-
-            @pl.when((s // layers != d) & jnp.logical_not(passed_on))
+            @pl.when(s // layers != d)
             def _():
-                window_copy(s, relay_s.at[0], partner).wait_recv()
+                into_window(V.at[s], s, send_v.at[0, 0], g, partner).wait_recv()
 
         def enter(s):
             c, n = sincos(V[s])
@@ -279,11 +319,16 @@
             @pl.when(s // per == y)
             def _():
                 slot = s % per
-                dbuf[slot] = -0.5 * (qr * us[slot, 1] + qi * us[slot, 0])
+                tall = select_left(row_back, -0.5 * (qr * us[slot, 1] + qi * us[slot, 0]))
+                dep_out[0, slot] = tall[:strip]
+                edge_copy(0, slot).start()
+                dep_out[1, slot] = tall[2 * strip :]
+                edge_copy(1, slot).start()
+                dep_mid[slot] = tall[strip : 2 * strip]
 
                 @pl.when(slot // layers != xl)
                 def _():
-                    gradient_copy(slot).start()
+                    middle_copy(slot).start()
 
         @pl.loop(0, slices - 1)
         def _(s):
@@ -307,49 +352,41 @@
             ps[1] = qi
             leave(s, qr, qi)
 
-    dep_copy = [
-        [remote(dep_out.at[n, s], dep_in.at[1 - n, s], dep_ss.at[n, s], dep_rs.at[1 - n, s], near[n]) for s in range(layers)]
-        for n in (0, 1)
-    ]
     for s in (1, 0):
         slot = layers * xl + s
 
         @pl.when(jnp.logical_not(active))
         def _():
-            gradient_copy(slot).wait_recv()
-
-        tall = select_left(row_back, dbuf[slot])
-        dep_out[0, s] = tall[:strip]
-        dep_copy[0][s].start()
-        dep_out[1, s] = tall[2 * strip :]
-        dep_copy[1][s].start()
-        o_ref[s] = spread(tall[strip : 2 * strip], pick[2])
-    for s in (1, 0):
+            middle_copy(slot).wait_recv()
+
+        total = spread(dep_mid[slot], pick[2])
         for n in (0, 1):
-            dep_copy[1 - n][s].wait_recv()
-            o_ref[s] += spread(dep_in[n, s], pick[n])
+            edge_copy(1 - n, slot).wait_recv()
+            total += spread(dep_in[n, s], pick[n])
+        o_ref[s] = total
 
     for n in (0, 1):
         pos_copy[n].wait_send()
         for s in range(layers):
             halo_copy[n][s].wait_send()
-            dep_copy[n][s].wait_send()
-    for s in range(layers):
-        mine = layers * d + s
-        window_copy(mine, send_v.at[0, s], up).wait_send()
-        window_copy(mine, send_v.at[1, s], down).wait_send()
 
     @pl.when(jnp.logical_not(active))
     def _():
         for s in range(layers):
-            window_copy(layers * d + s, send_v.at[2, s], partner).wait_send()
+            other_send(s).wait_send()
+        for k, copies in passing():
+            for copy in copies:
+                copy.wait_send()
 
     @pl.when(active)
     def _():
-        for k in range(4):
-            window_copy(0, relay_s.at[k], up).wait_send()
         for s in range(layers):
-            gradient_copy(layers * (1 - xl) + s).wait_send()
+            for copy in own_sends(s):
+                copy.wait_send()
+            middle_copy(layers * (1 - xl) + s).wait_send()
+        for slot in range(per):
+            for n in (0, 1):
+                edge_copy(n, slot).wait_send()
 
 
 def local(potential, probe, positions, intensity):
@@ -367,21 +404,22 @@
         out_specs=vm,
         scratch_shapes=[
             pltpu.VMEM((slices, W, W), f32),
+            pltpu.VMEM((6, W, W), f32),
             pltpu.VMEM((slices, 2, W, W), f32),
             pltpu.VMEM((2 * layers, 2, W, W), f32),
             pltpu.VMEM((2, W, W), f32),
-            pltpu.VMEM((2 * layers, W, W), f32),
             pltpu.VMEM((2, 8, 128), jnp.int32),
             pltpu.VMEM((2, 2, 8, 128), jnp.int32),
             pltpu.VMEM((2, layers, strip, W), f32),
             pltpu.VMEM((2, layers, strip, W), f32),
-            pltpu.VMEM((2, layers, strip, W), f32),
+            pltpu.VMEM((2, 2 * layers, strip, W), f32),
+            pltpu.VMEM((2 * layers, strip, W), f32),
             pltpu.VMEM((2, layers, strip, W), f32),
             pltpu.VMEM((layers, strip, W), f32),
             pltpu.VMEM((3, columns, W), bf16),
             dma((2,)), dma((2,)), dma((2, layers)), dma((2, layers)),
-            dma((3, layers)), dma((slices,)), dma((4,)), dma((2,)), dma((2,)),
-            dma((2, layers)), dma((2, layers)),
+            dma((layers, 2)), dma((slices,)), dma((6, 3)), dma((6,)),
+            dma((2, 2 * layers)), dma((2, layers)), dma((layers,)), dma((layers,)),
         ],
         compiler_params=pltpu.CompilerParams(
             collective_id=0, has_side_effects=True, vmem_limit_bytes=56 << 20

time: 97.7 us -> 79.2 us (0.81)
  the two profiles are of different devices: /device:TPU:0 before, /device:TPU:16 now
where the time goes in v3:
time: 79.2 us; the launch traced here: 79.1 us
  Pallas kernels  76.8 us (97%)
  local copies, waits for them, and re-layouts  2.31 us (3%)
    pallas_call x1, Pallas kernels, local(): pl.pallas_call(functools.partial(kernel, groups, depths), out_shape=jax.S...  76.8 us
    unnamed x1, local copies, waits for them, and re-layouts  2.31 us

profile of v3, /device:TPU:16, one launch (start us, length us, event | category | flops | bytes accessed | tf_op | source)
XLA Modules:
  0.0 79.1 jit_solution(1054656710161534719)
XLA Ops:
  0.0 76.8 %shard_map.64 = f32[2,128,1024]{2,1,0:T(8,128)} custom-call(f32[2,128,1024]{2,1,0:T(8,128)} %v_ref.1, f32[2,256,256]{2,1,0:T(8,128)} %p_ref.1, s32[1,2]{1,0:T(1,128)} %pos_ref.1, f32[1,256,256]{2,1,0:T(8,128)} %i_ref.1, bf16[2,4,256,256]{3,2,1,0:T(8,128)(2,1)} %constant.4.clone.T, bf16[2,4,256,256]{3,2,1,0:T(8,128)(2,1)} %constant.5.clone.Fr), custom_call_target="tpu_custom_call" | custom-call | tf_op jit(solution)/shard_map/pallas_call | solution.py:400
  76.8 2.3 %copy.8 = f32[2,128,1024]{2,1,0:T(8,128)} copy(f32[2,128,1024]{2,1,0:T(8,128)} %shard_map.64) | data formatting | bytes 2097152

commit v4 on v3

--- a/solution.py
+++ b/solution.py
@@ -102,27 +102,20 @@
     return cmm_left(Fr[0,0],Fr[1,0],Fr[0,1],Fr[1,1],yr,yi)
 
 
-def exact_parts(x):
-    high = x.astype(bf16)
-    rest = x - high.astype(f32)
-    mid = rest.astype(bf16)
-    return high, mid, (rest - mid.astype(f32)).astype(bf16)
-
-
 def select_right(x, chosen):
-    a, b, c = exact_parts(x)
-    return dot(a, chosen) + dot(b, chosen) + dot(c, chosen)
+    high, low = split(x)
+    return dot(high, chosen) + dot(low, chosen)
 
 
 def select_left(chosen, x):
-    a, b, c = exact_parts(x)
-    return dot(chosen, a) + dot(chosen, b) + dot(chosen, c)
+    high, low = split(x)
+    return dot(chosen, high) + dot(chosen, low)
 
 
 def spread(x, chosen):
     return sum(
         lax.dot_general(part, chosen, (((1,), (1,)), ((), ())), preferred_element_type=f32)
-        for part in exact_parts(x)
+        for part in split(x)
     )
 
 
@@ -140,11 +133,11 @@
 
 
 def kernel(
-    groups, depths, v_ref, p_ref, pos_ref, i_ref, T, Fr, o_ref,
-    V, held, cs, us, ps, pos_out, pos_in, halo_out, halo_in, dep_out, dep_mid, dep_in, own_cut, pick,
-    pos_ss, pos_rs, halo_ss, halo_rs, send_v, recv_v, held_s, held_r, dep_ss, dep_rs, mid_s, mid_r,
+    groups, depths, v_hbm, p_hbm, pos_ref, i_hbm, T_hbm, Fr_hbm, o_ref,
+    V, held, wave_in, wave_out, cs, us, ps, pos_out, pos_in, halo_out, halo_in, dep_out, dep_mid, dep_in, own_cut, pick,
+    pos_ss, pos_rs, halo_ss, halo_rs, send_v, recv_v, held_s, held_r, dep_ss, dep_rs, mid_s, mid_r, wave_s, wave_r, v_ref, p_ref, i_ref, T, Fr, load_s,
 ):
-    layers, strip, columns = v_ref.shape
+    layers, strip, columns = v_hbm.shape
     slices = layers * depths
     rows = groups * strip
     g = lax.axis_index("probe")
@@ -165,8 +158,18 @@
     peers = [there(near_by, at) for near_by in (before, after) for at in (d, partner)]
     peers += [there(g, partner)]
     peers += [there(near_by, at) for near_by in (g, beside) for at in (up, down)]
+    across = (d + depths // 2) % depths
+    peers += [there(g, across)]
     for peer in peers:
         pl.semaphore_signal(barrier, inc=1, device_id=peer, device_id_type=pl.DeviceIdType.MESH)
+    loads = [
+        pltpu.make_async_copy(source, target, load_s.at[k])
+        for k, (source, target) in enumerate(
+            [(v_hbm, v_ref), (p_hbm, p_ref), (i_hbm, i_ref), (T_hbm, T), (Fr_hbm, Fr)]
+        )
+    ]
+    for load in loads:
+        load.start()
     pos_out[0] = jnp.full((8, 128), pos_ref[0, 0], jnp.int32)
     pos_out[1] = jnp.full((8, 128), pos_ref[0, 1], jnp.int32)
     pl.semaphore_wait(barrier, len(peers))
@@ -189,6 +192,8 @@
         return ones_where(lines == place + wide(left, W))
 
     pick[2] = column_pick(pos_out[1][:1])
+    for load in loads:
+        load.wait()
     for s in range(layers):
         own_cut[s] = select_right(v_ref[s], pick[2])
     fold = ones_where(lax.broadcasted_iota(jnp.int32, (W, W), 0) == folded((W, W), 1))
@@ -220,20 +225,34 @@
     def into_held(source, k, sent, probe_at, depth_at):
         return remote(source, held.at[k], sent, held_r.at[k], there(probe_at, depth_at))
 
+    def needs(target, group):
+        target, group = (target + 4) % 4, (group + 4) % 4
+        return (target < 2) | ((target == 2) & (group == 3))
+
     def own_sends(s):
         mine = layers * d + s
         if s == 0:
             return (
-                into_held(V.at[mine], 2, send_v.at[s, 0], beside, up),
-                into_window(V.at[mine], mine, send_v.at[s, 1], g, down),
+                (needs(y + 2, y), into_held(V.at[mine], 2, send_v.at[s, 0], beside, up)),
+                (needs(y + 1, y) & ~needs(y + 2, y), into_window(V.at[mine], mine, send_v.at[s, 0], g, up)),
+                (needs(y - 1, y), into_window(V.at[mine], mine, send_v.at[s, 1], g, down)),
             )
         return (
-            into_window(V.at[mine], mine, send_v.at[s, 0], g, up),
-            into_held(V.at[mine], 4, send_v.at[s, 1], beside, down),
+            (needs(y - 2, y), into_held(V.at[mine], 4, send_v.at[s, 1], beside, down)),
+            (needs(y - 1, y) & ~needs(y - 2, y), into_window(V.at[mine], mine, send_v.at[s, 1], g, down)),
+            (needs(y + 1, y), into_window(V.at[mine], mine, send_v.at[s, 0], g, up)),
         )
 
     def other_send(s):
         return into_held(V.at[layers * d + s], s, send_v.at[s, 0], beside, partner)
+
+    def start_each(pairs):
+        for condition, copy in pairs:
+            pl.when(condition)(copy.start)
+
+    def end_each(pairs):
+        for condition, copy in pairs:
+            pl.when(condition)(copy.wait_send)
 
     for s in range(layers):
         mine = layers * d + s
@@ -244,8 +263,17 @@
 
         @pl.when(active)
         def _():
-            for copy in own_sends(s):
-                copy.start()
+            copies = own_sends(s)
+            if s == 0:
+                start_each(copies[:2])
+                pl.when(copies[2][0] & (y != 2))(copies[2][1].start)
+            else:
+                start_each(copies)
+
+                @pl.when(y == 2)
+                def _():
+                    copies[0][1].wait_send()
+                    own_sends(0)[2][1].start()
 
         @pl.when(jnp.logical_not(active))
         def _():
@@ -256,30 +284,66 @@
     def passing():
         low, high = (partner + depths - 2) % depths, (partner + 2) % depths
 
-        def sends(k, slice_at, *targets):
-            out = [into_window(held.at[k], slice_at, held_s.at[k, 0], beside, d)]
-            for n, (what, where) in enumerate(targets):
-                if what is None:
-                    out.append(into_window(held.at[k], slice_at, held_s.at[k, n + 1], beside, where))
-                else:
-                    out.append(into_held(held.at[k], what, held_s.at[k, n + 1], g, where))
-            return k, out
-
+        always = y >= 0
+
+        def home(k, slice_at, condition):
+            return condition, into_window(held.at[k], slice_at, held_s.at[k, 0], beside, d)
+
+        def window(k, slice_at, condition, where):
+            return condition, into_window(held.at[k], slice_at, held_s.at[k, 1], beside, where)
+
+        def direct(k, slice_at, condition, where):
+            return condition, into_window(held.at[k], slice_at, held_s.at[k, 2], beside, where)
+
+        def onward(k, to, condition, where):
+            return condition, into_held(held.at[k], to, held_s.at[k, 2], g, where)
+
+        first, second = layers * partner, layers * partner + 1
+        to_up, to_down = needs(y + 1, y - 1), needs(y - 1, y + 1)
+        here_low, here_high = needs(y, y - 1), needs(y, y + 1)
+        own_low, own_high = layers * down, layers * up + 1
+        part_low, part_high = layers * low, layers * high + 1
         return (
-            sends(0, layers * partner, (3, up), (None, down)),
-            sends(2, layers * down, (None, up)),
-            sends(4, layers * up + 1, (None, down)),
-            sends(1, layers * partner + 1, (None, up), (5, down)),
-            sends(3, layers * low, (None, up)),
-            sends(5, layers * high + 1, (None, down)),
+            (0, always, (
+                onward(0, 3, needs(y + 2, y), up), direct(0, first, needs(y + 1, y) & ~needs(y + 2, y), up),
+                window(0, first, needs(y - 1, y), down), home(0, first, always))),
+            (1, always, (
+                onward(1, 5, needs(y - 2, y), down), direct(1, second, needs(y - 1, y) & ~needs(y - 2, y), down),
+                window(1, second, needs(y + 1, y), up), home(1, second, always))),
+            (2, to_up, (window(2, own_low, to_up, up), home(2, own_low, to_up & here_low))),
+            (4, to_down, (window(4, own_high, to_down, down), home(4, own_high, to_down & here_high))),
+            (3, to_up, (window(3, part_low, to_up, up), home(3, part_low, to_up & here_low))),
+            (5, to_down, (window(5, part_high, to_down, down), home(5, part_high, to_down & here_high))),
         )
 
     @pl.when(jnp.logical_not(active))
     def _():
-        for k, copies in passing():
-            into_held(held.at[k], k, held_s.at[k, 0], beside, d).wait_recv()
-            for copy in copies:
-                copy.start()
+        for k, comes, copies in passing():
+            @pl.when(comes)
+            def _():
+                into_held(held.at[k], k, held_s.at[k, 0], beside, d).wait_recv()
+                if k == 0:
+                    pl.when(copies[2][0] & (y != 2))(copies[2][1].start)
+                    pl.when(copies[0][0] & (y != 3))(copies[0][1].start)
+                    start_each(copies[1:2] + copies[3:])
+                elif k == 1:
+                    pl.when(copies[2][0] & (y != 3))(copies[2][1].start)
+                    start_each(copies[:2] + copies[3:])
+                else:
+                    start_each(copies)
+
+                if k == 3:
+                    @pl.when(y == 3)
+                    def _():
+                        copies[0][1].wait_send()
+                        passing()[0][2][0][1].start()
+                        passing()[1][2][2][1].start()
+
+            if k == 1:
+                @pl.when(y == 2)
+                def _():
+                    copies[0][1].wait_send()
+                    passing()[0][2][2][1].start()
 
     def edge_copy(n, slot):
         return remote(
@@ -301,10 +365,34 @@
             def _():
                 into_window(V.at[s], s, send_v.at[0, 0], g, partner).wait_recv()
 
-        def enter(s):
+        def prepare(s):
+            arrive(s)
             c, n = sincos(V[s])
             cs[s, 0] = c
             cs[s, 1] = n
+
+        ready = jnp.where(y == 0, 0, per * y)
+        ready_end = jnp.where(y == 0, 0, jnp.where(y == 2, slices, per * (y + 1)))
+
+        def wave_copy(k, to, where):
+            return remote(wave_out.at[k], wave_in.at[to], wave_s.at[k], wave_r.at[to], there(g, where))
+
+        @pl.loop(ready, ready_end)
+        def _(s):
+            prepare(s)
+
+        @pl.when(y >= 2)
+        def _():
+            for c in (0, 1):
+                wave_copy(c, c, down).wait_recv()
+                ps[c] = wave_in[c]
+
+        def enter(s):
+            @pl.when((s < ready) | (s >= ready_end))
+            def _():
+                prepare(s)
+
+            c, n = cs[s, 0], cs[s, 1]
             ar, ai = ps[0], ps[1]
             ur, ui = c * ar - n * ai, c * ai + n * ar
 
@@ -330,15 +418,39 @@
                 def _():
                     middle_copy(slot).start()
 
-        @pl.loop(0, slices - 1)
+        @pl.loop(jnp.where(y < 2, 0, per * y), slices - 1)
         def _(s):
-            arrive(s)
             ur, ui = enter(s)
             ps[0], ps[1] = propagate(ur, ui, T)
 
-        arrive(slices - 1)
+            @pl.when((y == 1) & (s == 2 * per - 1))
+            def _():
+                wave_out[0] = ps[0]
+                wave_copy(0, 0, up).start()
+
+            @pl.when((y == 0) & (s == 2 * per - 1))
+            def _():
+                wave_out[0] = ps[1]
+                wave_copy(0, 1, across).start()
+
+            @pl.when((y == 0) & (s == 3 * per - 1))
+            def _():
+                for c in (0, 1):
+                    wave_out[1 + c] = ps[c]
+                    wave_copy(1 + c, c, down).start()
+
         ur, ui = enter(slices - 1)
         qr, qi = detector(ur, ui, i_ref[0], Fr)
+
+        @pl.when(y < 2)
+        def _():
+            wave_copy(0, 0, up).wait_send()
+
+        @pl.when(y == 0)
+        def _():
+            for c in (0, 1):
+                wave_copy(1 + c, c, down).wait_send()
+
         ps[0] = qr
         ps[1] = qi
         leave(slices - 1, qr, qi)
@@ -374,15 +486,25 @@
     def _():
         for s in range(layers):
             other_send(s).wait_send()
-        for k, copies in passing():
-            for copy in copies:
-                copy.wait_send()
+        for k, comes, copies in passing():
+            if k == 1:
+                end_each(copies[1:])
+                pl.when(copies[0][0] & (y != 2))(copies[0][1].wait_send)
+            elif k == 3:
+                end_each(copies[1:])
+                pl.when(copies[0][0] & (y != 3))(copies[0][1].wait_send)
+            else:
+                end_each(copies)
 
     @pl.when(active)
     def _():
         for s in range(layers):
-            for copy in own_sends(s):
-                copy.wait_send()
+            copies = own_sends(s)
+            if s == 0:
+                end_each(copies)
+            else:
+                end_each(copies[1:])
+                pl.when(copies[0][0] & (y != 2))(copies[0][1].wait_send)
             middle_copy(layers * (1 - xl) + s).wait_send()
         for slot in range(per):
             for n in (0, 1):
@@ -396,15 +518,18 @@
     slices = layers * depths
     T, Fr = tables()
     vm = pl.BlockSpec(memory_space=pltpu.VMEM)
+    far = pl.BlockSpec(memory_space=pl.ANY)
     dma = pltpu.SemaphoreType.DMA
     return pl.pallas_call(
         functools.partial(kernel, groups, depths),
         out_shape=jax.ShapeDtypeStruct(potential.shape, f32),
-        in_specs=[vm, vm, pl.BlockSpec(memory_space=pltpu.SMEM), vm, vm, vm],
+        in_specs=[far, far, pl.BlockSpec(memory_space=pltpu.SMEM), far, far, far],
         out_specs=vm,
         scratch_shapes=[
             pltpu.VMEM((slices, W, W), f32),
             pltpu.VMEM((6, W, W), f32),
+            pltpu.VMEM((2, W, W), f32),
+            pltpu.VMEM((3, W, W), f32),
             pltpu.VMEM((slices, 2, W, W), f32),
             pltpu.VMEM((2 * layers, 2, W, W), f32),
             pltpu.VMEM((2, W, W), f32),
@@ -420,6 +545,13 @@
             dma((2,)), dma((2,)), dma((2, layers)), dma((2, layers)),
             dma((layers, 2)), dma((slices,)), dma((6, 3)), dma((6,)),
             dma((2, 2 * layers)), dma((2, layers)), dma((layers,)), dma((layers,)),
+            dma((3,)), dma((2,)),
+            pltpu.VMEM(potential.shape, f32),
+            pltpu.VMEM(probe.shape, f32),
+            pltpu.VMEM(intensity.shape, f32),
+            pltpu.VMEM(T.shape, bf16),
+            pltpu.VMEM(Fr.shape, bf16),
+            dma((5,)),
         ],
         compiler_params=pltpu.CompilerParams(
             collective_id=0, has_side_effects=True, vmem_limit_bytes=56 << 20

time: 79.2 us -> 74 us (0.934)
  the two profiles are of different devices: /device:TPU:16 before, /device:TPU:1 now
where the time goes in v4:
time: 74 us; the launch traced here: 73.8 us
  Pallas kernels  71.5 us (97%)
  local copies, waits for them, and re-layouts  2.31 us (3%)
    pallas_call x1, Pallas kernels, local(): pl.pallas_call(functools.partial(kernel, groups, depths), out_shape=jax.S...  71.5 us
    unnamed x1, local copies, waits for them, and re-layouts  2.31 us

profile of v4, /device:TPU:1, one launch (start us, length us, event | category | flops | bytes accessed | tf_op | source)
XLA Modules:
  0.0 73.8 jit_solution(3054798971885921664)
XLA Ops:
  0.0 71.5 %shard_map.64 = f32[2,128,1024]{2,1,0:T(8,128)} custom-call(f32[2,128,1024]{2,1,0:T(8,128)} %v_hbm.1, f32[2,256,256]{2,1,0:T(8,128)} %p_hbm.1, s32[1,2]{1,0:T(1,128)} %pos_ref.1, f32[1,256,256]{2,1,0:T(8,128)} %i_hbm.1, bf16[2,4,256,256]{3,2,1,0:T(8,128)(2,1)} %constant.4.clone.T_hbm, bf16[2,4,256,256]{3,2,1,0:T(8,128)(2,1)} %constant.5.clone.Fr_hbm), custom_call_target="tpu_custom_call" | custom-call | tf_op jit(solution)/shard_map/pallas_call | solution.py:523
  71.5 2.3 %copy.8 = f32[2,128,1024]{2,1,0:T(8,128)} copy(f32[2,128,1024]{2,1,0:T(8,128)} %shard_map.64) | data formatting | bytes 2097152

commit v5 on v4

--- a/solution.py
+++ b/solution.py
@@ -37,10 +37,15 @@
         left=np.block([[B.real,-B.imag],[B.imag,B.real]])
         out.append((right,left))
     prop=[out[0][0],out[1][0],out[0][1],out[1][1]]
-    G=F[:,order]
-    far=[G.T.real,G.T.imag,G.real,G.imag]
-    hp,lp=zip(*[halves(a) for a in prop]); hf,lf=zip(*[halves(a) for a in far])
-    return np.stack([np.stack(hp),np.stack(lp)]), np.stack([np.stack(hf),np.stack(lf)])
+    half=np.arange(HB)+.5
+    turn=2*np.pi/W*half[:,None]*half[None,:]
+    zero=np.zeros((HB,HB))
+    waves=np.block([[np.cos(turn),zero],[zero,np.sin(turn)]])/np.sqrt(W)
+    shift=np.exp(2j*np.pi*(order/(2*W)+1/(8*W)))
+    phase=shift[:,None]*shift[None,:]
+    hp,lp=zip(*[halves(a) for a in prop])
+    return (np.stack([np.stack(hp),np.stack(lp)]), np.stack(halves(waves)),
+            np.stack([phase.real,phase.imag]).astype(np.float32))
 
 def split(x):
     hi=x.astype(bf16)
@@ -51,10 +56,12 @@
 
 def mm_right(x, wh, wl):
     h,l=split(x)
-    return dot(h,wh)+dot(l,wh)+dot(h,wl)
+    y=dot(jnp.concatenate([h,l],0),wh)
+    return y[:W]+y[W:]+dot(h,wl)
 def mm_left(wh,wl,x):
     h,l=split(x)
-    return dot(wh,h)+dot(wh,l)+dot(wl,h)
+    y=dot(jnp.concatenate([wh,wl],0),h)
+    return y[:W]+y[W:]+dot(wh,l)
 
 def propagate(ur,ui,T):
     ure,uro=ur[:,:HB]+ur[:,HB:],ur[:,:HB]-ur[:,HB:]
@@ -73,16 +80,19 @@
                                 jnp.concatenate([b[:,:HB]+b[:,HB:],b[:,:HB]-b[:,HB:]],1)],0)
     return unfold(top[:HB],bot[:HB]),unfold(top[HB:],bot[HB:])
 
-def cmm_right(xr,xi,rh,rl,ih,il):
-    hr,lr=split(xr); hi,li=split(xi)
-    yr=dot(hr,rh)+dot(lr,rh)+dot(hr,rl)-(dot(hi,ih)+dot(li,ih)+dot(hi,il))
-    yi=dot(hr,ih)+dot(lr,ih)+dot(hr,il)+(dot(hi,rh)+dot(li,rh)+dot(hi,rl))
-    return yr,yi
-def cmm_left(rh,rl,ih,il,xr,xi):
-    hr,lr=split(xr); hi,li=split(xi)
-    yr=dot(rh,hr)+dot(rh,lr)+dot(rl,hr)-(dot(ih,hi)+dot(ih,li)+dot(il,hi))
-    yi=dot(ih,hr)+dot(ih,lr)+dot(il,hr)+(dot(rh,hi)+dot(rh,li)+dot(rl,hi))
-    return yr,yi
+def shifted_right(xr,xi,w):
+    def parts(x):
+        p=mm_right(jnp.concatenate([x[:,:HB]-x[:,HB:],x[:,:HB]+x[:,HB:]],1),w[0],w[1])
+        return p[:,:HB],p[:,HB:]
+    (ar,br),(ai,bi)=parts(xr),parts(xi)
+    return jnp.concatenate([bi+ar,bi-ar],1),jnp.concatenate([ai-br,-ai-br],1)
+
+def shifted_left(w,xr,xi):
+    def parts(x):
+        p=mm_left(w[0],w[1],jnp.concatenate([x[:HB]-x[HB:],x[:HB]+x[HB:]],0))
+        return p[:HB],p[HB:]
+    (ar,br),(ai,bi)=parts(xr),parts(xi)
+    return jnp.concatenate([bi+ar,bi-ar],0),jnp.concatenate([ai-br,-ai-br],0)
 
 def poly(c,z):
     r=jnp.full_like(z,float(c[-1]))
@@ -93,14 +103,14 @@
     x=0.5*v; z=x*x
     return poly(COSC,z), x*poly(SINC,z)
 
-def detector(ur,ui,inten,Fr):
-    yr,yi=cmm_right(ur,ui,Fr[0,0],Fr[1,0],Fr[0,1],Fr[1,1])
-    fr,fi=cmm_left(Fr[0,2],Fr[1,2],Fr[0,3],Fr[1,3],yr,yi)
-    m=fr*fr+fi*fi-inten
-    gr,gi=m*fr,-(m*fi)
-    yr,yi=cmm_right(gr,gi,Fr[0,2],Fr[1,2],Fr[0,3],Fr[1,3])
-    return cmm_left(Fr[0,0],Fr[1,0],Fr[0,1],Fr[1,1],yr,yi)
-
+def detector(ur,ui,inten,Fr,phase):
+    er,ei=phase[0],phase[1]
+    yr,yi=shifted_right(er*ur-ei*ui,er*ui+ei*ur,Fr)
+    vr,vi=shifted_left(Fr,yr,yi)
+    m=vr*vr+vi*vi-inten
+    yr,yi=shifted_right(m*vr,-(m*vi),Fr)
+    zr,zi=shifted_left(Fr,yr,yi)
+    return er*zr-ei*zi,er*zi+ei*zr
 
 def select_right(x, chosen):
     high, low = split(x)
@@ -133,9 +143,9 @@
 
 
 def kernel(
-    groups, depths, v_hbm, p_hbm, pos_ref, i_hbm, T_hbm, Fr_hbm, o_ref,
+    groups, depths, v_hbm, p_hbm, pos_ref, i_hbm, T_hbm, Fr_hbm, phase_hbm, o_ref,
     V, held, wave_in, wave_out, cs, us, ps, pos_out, pos_in, halo_out, halo_in, dep_out, dep_mid, dep_in, own_cut, pick,
-    pos_ss, pos_rs, halo_ss, halo_rs, send_v, recv_v, held_s, held_r, dep_ss, dep_rs, mid_s, mid_r, wave_s, wave_r, v_ref, p_ref, i_ref, T, Fr, load_s,
+    pos_ss, pos_rs, halo_ss, halo_rs, send_v, recv_v, held_s, held_r, dep_ss, dep_rs, mid_s, mid_r, wave_s, wave_r, v_ref, p_ref, i_ref, T, Fr, phase, load_s,
 ):
     layers, strip, columns = v_hbm.shape
     slices = layers * depths
@@ -165,7 +175,7 @@
     loads = [
         pltpu.make_async_copy(source, target, load_s.at[k])
         for k, (source, target) in enumerate(
-            [(v_hbm, v_ref), (p_hbm, p_ref), (i_hbm, i_ref), (T_hbm, T), (Fr_hbm, Fr)]
+            [(v_hbm, v_ref), (p_hbm, p_ref), (i_hbm, i_ref), (T_hbm, T), (Fr_hbm, Fr), (phase_hbm, phase)]
         )
     ]
     for load in loads:
@@ -199,6 +209,7 @@
     fold = ones_where(lax.broadcasted_iota(jnp.int32, (W, W), 0) == folded((W, W), 1))
     for c in (0, 1):
         ps[c] = select_left(fold, select_right(p_ref[c], fold))
+    i_ref[0] = select_left(fold, select_right(i_ref[0], fold))
     offset = (pos_out[0][:1] - (g - 1) * strip + rows) & (rows - 1)
     row_pick = ones_where(
         lax.broadcasted_iota(jnp.int32, (W, 3 * strip), 1) == folded((W, 3 * strip), 0) + wide(offset, 3 * strip)
@@ -371,8 +382,8 @@
             cs[s, 0] = c
             cs[s, 1] = n
 
-        ready = jnp.where(y == 0, 0, per * y)
-        ready_end = jnp.where(y == 0, 0, jnp.where(y == 2, slices, per * (y + 1)))
+        ready = jnp.where(y == 0, layers * core, per * y)
+        ready_end = jnp.where(y == 0, 2 * layers * core, jnp.where(y == 2, slices, per * (y + 1)))
 
         def wave_copy(k, to, where):
             return remote(wave_out.at[k], wave_in.at[to], wave_s.at[k], wave_r.at[to], there(g, where))
@@ -440,7 +451,7 @@
                     wave_copy(1 + c, c, down).start()
 
         ur, ui = enter(slices - 1)
-        qr, qi = detector(ur, ui, i_ref[0], Fr)
+        qr, qi = detector(ur, ui, i_ref[0], Fr, phase)
 
         @pl.when(y < 2)
         def _():
@@ -516,14 +527,14 @@
     groups = lax.axis_size("probe")
     depths = lax.axis_size("depth")
     slices = layers * depths
-    T, Fr = tables()
+    T, Fr, phase = tables()
     vm = pl.BlockSpec(memory_space=pltpu.VMEM)
     far = pl.BlockSpec(memory_space=pl.ANY)
     dma = pltpu.SemaphoreType.DMA
     return pl.pallas_call(
         functools.partial(kernel, groups, depths),
         out_shape=jax.ShapeDtypeStruct(potential.shape, f32),
-        in_specs=[far, far, pl.BlockSpec(memory_space=pltpu.SMEM), far, far, far],
+        in_specs=[far, far, pl.BlockSpec(memory_space=pltpu.SMEM), far, far, far, far],
         out_specs=vm,
         scratch_shapes=[
             pltpu.VMEM((slices, W, W), f32),
@@ -551,12 +562,13 @@
             pltpu.VMEM(intensity.shape, f32),
             pltpu.VMEM(T.shape, bf16),
             pltpu.VMEM(Fr.shape, bf16),
-            dma((5,)),
+            pltpu.VMEM(phase.shape, f32),
+            dma((6,)),
         ],
         compiler_params=pltpu.CompilerParams(
             collective_id=0, has_side_effects=True, vmem_limit_bytes=56 << 20
         ),
-    )(potential, probe, positions, intensity, jnp.asarray(T), jnp.asarray(Fr))
+    )(potential, probe, positions, intensity, jnp.asarray(T), jnp.asarray(Fr), jnp.asarray(phase))
 
 
 def solution(mesh):

time: 74 us -> 73.7 us (level)
  no operation moved by 1% of the time
where the time goes in v5:
time: 73.7 us; the launch traced here: 73.6 us
  Pallas kernels  71.3 us (97%)
  local copies, waits for them, and re-layouts  2.31 us (3%)
    pallas_call x1, Pallas kernels, local(): pl.pallas_call(functools.partial(kernel, groups, depths), out_shape=jax.S...  71.3 us
    unnamed x1, local copies, waits for them, and re-layouts  2.31 us

profile of v5, /device:TPU:1, one launch (start us, length us, event | category | flops | bytes accessed | tf_op | source)
XLA Modules:
  0.0 73.6 jit_solution(10982080708831188646)
XLA Ops:
  0.0 71.3 %shard_map.73 = f32[2,128,1024]{2,1,0:T(8,128)} custom-call(f32[2,128,1024]{2,1,0:T(8,128)} %v_hbm.1, f32[2,256,256]{2,1,0:T(8,128)} %p_hbm.1, s32[1,2]{1,0:T(1,128)} %pos_ref.1, f32[1,256,256]{2,1,0:T(8,128)} %i_hbm.1, bf16[2,4,256,256]{3,2,1,0:T(8,128)(2,1)} %constant.6.clone.T_hbm, bf16[2,256,256]{2,1,0:T(8,128)(2,1)} %constant.7.clone.Fr_hbm, ...), custom_call_target="tpu_custom_call" | custom-call | tf_op jit(solution)/shard_map/pallas_call | solution.py:534
  71.3 2.3 %copy.9 = f32[2,128,1024]{2,1,0:T(8,128)} copy(f32[2,128,1024]{2,1,0:T(8,128)} %shard_map.73) | data formatting | bytes 2097152

commit v6 on v5

--- a/solution.py
+++ b/solution.py
@@ -222,13 +222,14 @@
         [remote(halo_out.at[n, s], halo_in.at[1 - n, s], halo_ss.at[n, s], halo_rs.at[1 - n, s], near[n]) for s in range(layers)]
         for n in (0, 1)
     ]
-    for n in (0, 1):
-        pos_copy[1 - n].wait_recv()
+    near_first = (1 - core, core)
+    for n in near_first:
+        remote(pos_out, pos_in.at[n], pos_ss.at[n], pos_rs.at[n], near[0]).wait_recv()
         pick[n] = column_pick(pos_in[n, 1][:1])
-    for s in range(layers):
-        for n in (0, 1):
+        to = there(jnp.where(n == 0, before, after), d)
+        for s in range(layers):
             halo_out[n, s] = select_right(v_ref[s], pick[n])
-            halo_copy[n][s].start()
+            remote(halo_out.at[n, s], halo_in.at[1 - n, s], halo_ss.at[n, s], halo_rs.at[1 - n, s], to).start()
 
     def into_window(source, slice_at, sent, probe_at, depth_at):
         return remote(source, V.at[slice_at], sent, recv_v.at[slice_at], there(probe_at, depth_at))
@@ -483,8 +484,8 @@
             middle_copy(slot).wait_recv()
 
         total = spread(dep_mid[slot], pick[2])
-        for n in (0, 1):
-            edge_copy(1 - n, slot).wait_recv()
+        for n in near_first:
+            remote(dep_out.at[n, slot], dep_in.at[n, s], dep_ss.at[n, slot], dep_rs.at[n, s], near[0]).wait_recv()
             total += spread(dep_in[n, s], pick[n])
         o_ref[s] = total
 

time: 73.7 us -> 73.5 us (level)
  no operation moved by 1% of the time
where the time goes in v6:
time: 73.5 us; the launch traced here: 73.3 us
  Pallas kernels  71 us (97%)
  local copies, waits for them, and re-layouts  2.31 us (3%)
    pallas_call x1, Pallas kernels, local(): pl.pallas_call(functools.partial(kernel, groups, depths), out_shape=jax.S...  71 us
    unnamed x1, local copies, waits for them, and re-layouts  2.31 us

profile of v6, /device:TPU:1, one launch (start us, length us, event | category | flops | bytes accessed | tf_op | source)
XLA Modules:
  0.0 73.3 jit_solution(16861002593498904819)
XLA Ops:
  0.0 71.0 %shard_map.73 = f32[2,128,1024]{2,1,0:T(8,128)} custom-call(f32[2,128,1024]{2,1,0:T(8,128)} %v_hbm.1, f32[2,256,256]{2,1,0:T(8,128)} %p_hbm.1, s32[1,2]{1,0:T(1,128)} %pos_ref.1, f32[1,256,256]{2,1,0:T(8,128)} %i_hbm.1, bf16[2,4,256,256]{3,2,1,0:T(8,128)(2,1)} %constant.6.clone.T_hbm, bf16[2,256,256]{2,1,0:T(8,128)(2,1)} %constant.7.clone.Fr_hbm, ...), custom_call_target="tpu_custom_call" | custom-call | tf_op jit(solution)/shard_map/pallas_call | solution.py:535
  71.0 2.3 %copy.9 = f32[2,128,1024]{2,1,0:T(8,128)} copy(f32[2,128,1024]{2,1,0:T(8,128)} %shard_map.73) | data formatting | bytes 2097152

commit v7 on v6

--- a/solution.py
+++ b/solution.py
@@ -347,7 +347,6 @@
                 if k == 3:
                     @pl.when(y == 3)
                     def _():
-                        copies[0][1].wait_send()
                         passing()[0][2][0][1].start()
                         passing()[1][2][2][1].start()
 
@@ -502,9 +501,6 @@
             if k == 1:
                 end_each(copies[1:])
                 pl.when(copies[0][0] & (y != 2))(copies[0][1].wait_send)
-            elif k == 3:
-                end_each(copies[1:])
-                pl.when(copies[0][0] & (y != 3))(copies[0][1].wait_send)
             else:
                 end_each(copies)
 

time: 73.5 us -> 73.5 us (level)
  no operation moved by 1% of the time
where the time goes in v7:
time: 73.5 us; the launch traced here: 73.3 us
  Pallas kernels  71 us (97%)
  local copies, waits for them, and re-layouts  2.31 us (3%)
    pallas_call x1, Pallas kernels, local(): pl.pallas_call(functools.partial(kernel, groups, depths), out_shape=jax.S...  71 us
    unnamed x1, local copies, waits for them, and re-layouts  2.31 us

profile of v7, /device:TPU:1, one launch (start us, length us, event | category | flops | bytes accessed | tf_op | source)
XLA Modules:
  0.0 73.3 jit_solution(3315088281470753769)
XLA Ops:
  0.0 71.0 %shard_map.73 = f32[2,128,1024]{2,1,0:T(8,128)} custom-call(f32[2,128,1024]{2,1,0:T(8,128)} %v_hbm.1, f32[2,256,256]{2,1,0:T(8,128)} %p_hbm.1, s32[1,2]{1,0:T(1,128)} %pos_ref.1, f32[1,256,256]{2,1,0:T(8,128)} %i_hbm.1, bf16[2,4,256,256]{3,2,1,0:T(8,128)(2,1)} %constant.6.clone.T_hbm, bf16[2,256,256]{2,1,0:T(8,128)(2,1)} %constant.7.clone.Fr_hbm, ...), custom_call_target="tpu_custom_call" | custom-call | tf_op jit(solution)/shard_map/pallas_call | solution.py:531
  71.0 2.3 %copy.9 = f32[2,128,1024]{2,1,0:T(8,128)} copy(f32[2,128,1024]{2,1,0:T(8,128)} %shard_map.73) | data formatting | bytes 2097152
